TPU v7x, 512 devices: a whole 4x4x16 slice. The times are simulated.
512 devices in a mesh: dp: 8 (over x, z_hi), ctx: 64 (over y, z_lo, core).
Axes of the slice: x: 4, y: 4, z: 16 (z_hi: 2, z_lo: 8; z = z_hi * 8 + z_lo), core: 2. Of those that a mesh axis runs over, the one named last changes fastest.
Arguments:
- student_hidden: bfloat16 [131072, 1024], P(('dp', 'ctx'))
- w_query: bfloat16 [1024, 1024], P('dp'), may hold values from -0.5 to 0.5
- w_keyval: bfloat16 [1024, 512], P('dp'), may hold values from -0.1875 to 0.1875
- w_out: bfloat16 [1024, 1024], P('dp'), may hold values from -0.1875 to 0.1875
- norm_gain: float32 [1024], replicated, may hold values from 0.1 to 1.9
- student_head: float32 [1024], replicated, may hold values from -0.6 to 0.6
- teacher_query: bfloat16 [32, 2048], P('dp')
- teacher_keys: bfloat16 [131072, 2048], P(('dp', 'ctx')), may hold values from -6 to 6
- teacher_values: bfloat16 [131072, 2048], P(('dp', 'ctx')), may hold values from -6 to 6
- teacher_head: float32 [2048], replicated, may hold values from -0.125 to 0.125
- thread_lengths: int32 [32], replicated, may hold values from 1024 to 4096, as said below
- list_index: int32 [32], replicated, may hold values from 0 to 7, as said below
- relevance: int32 [32], replicated, may hold values from 0 to 3
Outputs:
- student_out: float32 [131072, 1024], P(('dp', 'ctx'))
- pooled: float32 [32, 1024], P('dp')
- teacher_score: float32 [32], P('dp')
- divergence: float32 [8], replicated
Inputs may be any that keep to these rules, and one draw needn't show every extreme that they name: `thread_lengths`: each thread's valid tokens form its first rows; some thread is full and some has exactly 1024 valid tokens. `list_index`: each list holds exactly 4 threads.
All inputs are finite; a program needn't handle non-finite values.
Results may differ from a plain program's by a relative error of at most 0.007.
The roundings to bfloat16 on the way count: a program that leaves them out, or rounds other values in their place, can miss the bound.
Values may be sent and summed in bfloat16 or wider, within the bound.
A program may use at most 128 MiB of HBM per device.

v0:
```python
import jax
import jax.numpy as jnp
from jax import lax
from jax.sharding import PartitionSpec as P

HEADS = 8
KV_HEADS = 2
HD = 128
T_HEADS = 16


def shifted_2(value, axis, steps):
    count = lax.axis_size(axis)
    first, last = (max(0, -steps), min(count, count - steps))
    return lax.ppermute(value, axis, [(source, source + steps) for source in range(first, last)])


def joined(value, axis, join):
    pieces = jax.tree.map(lambda part: lax.all_gather(part, axis), value)
    head = jax.tree.map(lambda part: part[0], pieces)
    tail = jax.tree.map(lambda part: part[1:], pieces)
    running, _ = lax.scan(lambda running, section: (join(running, section), None), head, tail)
    return running


def normalize(hidden, gain):
    return hidden * lax.rsqrt(jnp.mean(hidden * hidden, axis=-1, keepdims=True) + 1e-05) * gain


def add_rows(left, piece):
    return jnp.dot(left, piece, preferred_element_type=jnp.float32)


def attend(state, queries, block, key_pos, query_pos, scale):
    best, total, accum = state
    width = KV_HEADS * HD
    keys = block[:, :width].reshape(block.shape[0], KV_HEADS, HD)
    values = block[:, width:].reshape(block.shape[0], KV_HEADS, HD)
    visible = (key_pos[None, :] >= 0) & (key_pos[None, :] <= query_pos[:, None])
    visible = visible[:, None, None, :]
    scores = jnp.einsum("qkgd,tkd->qkgt", queries, keys, preferred_element_type=jnp.float32) * scale
    scores = jnp.where(visible, scores, -1e30)
    fresh = jnp.maximum(best, jnp.max(scores, axis=-1))
    carry = jnp.exp(best - fresh)
    weights = jnp.where(visible, jnp.exp(scores - fresh[..., None]), 0.0)
    total = total * carry + jnp.sum(weights, axis=-1)
    accum = accum * carry[..., None] + jnp.einsum(
        "qkgt,tkd->qkgd", weights.astype(jnp.bfloat16), values, preferred_element_type=jnp.float32
    )
    return (fresh, total, accum)


def combine_parts(first, second):
    best = jnp.maximum(first[0], second[0])
    early = jnp.exp(first[0] - best)
    late = jnp.exp(second[0] - best)
    return (
        best,
        first[1] * early + second[1] * late,
        first[2] * early[..., None] + second[2] * late[..., None],
    )


def list_divergence(teacher_score, student_score, list_index, relevance, lists):
    target = teacher_score + relevance.astype(jnp.float32)
    member = jnp.arange(lists)[:, None] == list_index[None, :]

    def log_soft(logits):
        masked = jnp.where(member, logits[None, :], -1e30)
        top = jnp.max(masked, axis=1, keepdims=True)
        shifted = jnp.where(member, jnp.exp(masked - top), 0.0)
        return masked - top - jnp.log(jnp.sum(shifted, axis=1, keepdims=True))

    target_log = log_soft(target)
    student_log = log_soft(student_score)
    target_prob = jnp.where(member, jnp.exp(target_log), 0.0)
    return jnp.sum(jnp.where(member, target_prob * (target_log - student_log), 0.0), axis=1)


def local(
    student_hidden,
    w_query,
    w_keyval,
    w_out,
    norm_gain,
    student_head,
    teacher_query,
    teacher_keys,
    teacher_values,
    teacher_head,
    thread_lengths,
    list_index,
    relevance,
):
    rows, model_width = student_hidden.shape
    thread_devs = lax.axis_size("ctx") // 4
    loops = lax.axis_size("ctx") // thread_devs
    place = lax.axis_index("ctx")
    slot = place // thread_devs
    position = place % thread_devs
    own_threads = lax.axis_index("dp") * loops + jnp.arange(loops)
    every_thread = jnp.arange(thread_lengths.shape[0])
    own_lengths = jnp.sum(
        jnp.where(every_thread[None, :] == own_threads[:, None], thread_lengths[None, :], 0), axis=1
    )
    slot_mask = jnp.arange(loops) == slot
    length = jnp.sum(jnp.where(slot_mask, own_lengths, 0))
    query_pos = position * rows + jnp.arange(rows)
    valid = query_pos < length
    scale = HD ** (-0.5)
    groups = HEADS // KV_HEADS
    query_full = add_rows(student_hidden, lax.all_gather(w_query, "dp", axis=0, tiled=True))
    keyval_full = add_rows(student_hidden, lax.all_gather(w_keyval, "dp", axis=0, tiled=True))
    queries = query_full.astype(jnp.bfloat16).reshape(rows, KV_HEADS, groups, HD)
    keyval = keyval_full.astype(jnp.bfloat16)
    state = (
        jnp.full((rows, KV_HEADS, groups), -1e30, jnp.float32),
        jnp.zeros((rows, KV_HEADS, groups), jnp.float32),
        jnp.zeros((rows, KV_HEADS, groups, HD), jnp.float32),
    )
    state = attend(state, queries, keyval, query_pos, query_pos, scale)

    def step(turn, carried):
        block, inner = carried
        block = shifted_2(block, "ctx", 1)
        key_pos = (position - turn) * rows + jnp.arange(rows)
        return (block, attend(inner, queries, block, key_pos, query_pos, scale))

    ignored, state = lax.fori_loop(1, thread_devs, step, (keyval, state))
    best, total, accum = state
    attended = (accum / total[..., None]).reshape(rows, HEADS * HD).astype(jnp.bfloat16)
    mixed = add_rows(attended, lax.all_gather(w_out, "dp", axis=0, tiled=True))
    hidden = student_hidden.astype(jnp.float32) + mixed
    student_out = jnp.where(valid[:, None], hidden, 0.0)
    normed = normalize(hidden, norm_gain)
    pooled_part = jnp.sum(jnp.where(valid[:, None], normed, 0.0), axis=0)
    pool_slots = jnp.where(slot_mask[:, None], pooled_part[None, :], 0.0)
    own_query = jnp.sum(
        jnp.where(slot_mask[:, None], teacher_query.astype(jnp.float32), 0.0), axis=0
    ).astype(jnp.bfloat16)
    head_query = own_query.reshape(T_HEADS, HD)
    head_keys = teacher_keys.reshape(rows, T_HEADS, HD)
    head_values = teacher_values.reshape(rows, T_HEADS, HD)
    teacher_scores = (
        jnp.einsum("hd,thd->ht", head_query, head_keys, preferred_element_type=jnp.float32) * scale
    )
    teacher_scores = jnp.where(valid[None, :], teacher_scores, -1e30)
    teacher_best = jnp.max(teacher_scores, axis=-1)
    teacher_weights = jnp.where(
        valid[None, :], jnp.exp(teacher_scores - teacher_best[:, None]), 0.0
    )
    teacher_total = jnp.sum(teacher_weights, axis=-1)
    teacher_accum = jnp.einsum(
        "ht,thd->hd",
        teacher_weights.astype(jnp.bfloat16),
        head_values,
        preferred_element_type=jnp.float32,
    )
    best_slots = jnp.where(slot_mask[:, None], teacher_best[None, :], -1e30)
    total_slots = jnp.where(slot_mask[:, None], teacher_total[None, :], 0.0)
    accum_slots = jnp.where(slot_mask[:, None, None], teacher_accum[None, :, :], 0.0)
    best_all, total_all, accum_all = joined(
        (best_slots, total_slots, accum_slots), "ctx", combine_parts
    )
    pool_all = lax.psum(pool_slots, "ctx")
    teacher_out = (accum_all / total_all[..., None]).reshape(loops, T_HEADS * HD)
    teacher_score = jnp.sum(teacher_out * teacher_head[None, :], axis=1)
    pooled = pool_all / own_lengths.astype(jnp.float32)[:, None]
    student_score = jnp.sum(pooled * student_head[None, :], axis=1)
    teacher_every, student_every = (
        lax.all_gather(teacher_score, "dp", axis=0, tiled=True),
        lax.all_gather(student_score, "dp", axis=0, tiled=True),
    )
    threads = thread_lengths.shape[0]
    members = min(4, threads // 2)
    divergence = list_divergence(
        teacher_every, student_every, list_index, relevance, threads // members
    )
    return (student_out, pooled, teacher_score, divergence)


def solution(mesh):
    return jax.shard_map(
        local,
        mesh=mesh,
        in_specs=(
            P(("dp", "ctx"), None),
            P("dp", None),
            P("dp", None),
            P("dp", None),
            P(),
            P(),
            P("dp", None),
            P(("dp", "ctx"), None),
            P(("dp", "ctx"), None),
            P(),
            P(),
            P(),
            P(),
        ),
        out_specs=(P(("dp", "ctx"), None), P("dp", None), P("dp"), P()),
        check_vma=False,
    )
```

profile of v0, /device:TPU:8, one launch (start us, length us, event | category | flops | bytes accessed | tf_op | source)
XLA Modules:
  0.0 1032.4 jit_solution(17919914405679005430)
XLA Ops:
  14.8 124.9 %all_gather.31 = f32[64,4,16]{2,1,0:T(4,128)S(1)} all-gather(f32[1,4,16]{2,1,0:T(4,128)S(1)} %get-tuple-element.295), channel_id=1, replica_groups=mesh['dp'=8,'ctx'=64] {'ctx'}, dimensions={0}, use_global_device_ids=true | all-gather | bytes 16640 | tf_op jit(solution)/shard_map/all_gather | solution.py:19
  139.7 117.5 %all_gather.30 = f32[64,4,16]{2,1,0:T(4,128)S(1)} all-gather(f32[1,4,16]{2,1,0:T(4,128)S(1)} %get-tuple-element.296), channel_id=1, replica_groups=mesh['dp'=8,'ctx'=64] {'ctx'}, dimensions={0}, use_global_device_ids=true | all-gather | bytes 16640 | tf_op jit(solution)/shard_map/all_gather | solution.py:19
  262.0 2.3 convolution_convert_fusion
  269.1 315.0 %while.35 = (s32[]{:T(128)}, bf16[256,512]{0,1:T(8,128)(2,1)}, f32[256,2,4]{0,2,1:T(4,128)S(1)}, f32[256,2,4]{0,2,1:T(4,128)S(1)}, f32[256,2,4,128]{3,0,2,1:T(8,...) while((s32[]{:T(128)}, bf16[256,512]{0,1:T(8,128)(2,1)}, ...), condition=%wide.region_7.8_spmd.clone, body=%wide.region_4.7_spmd.clone.sunk | while | flops 275911680 | bytes 11670193 | solution.py:129
  269.1 2.2 collective-permute-start
  271.5 50.4 %collective-permute-done = bf16[256,512]{0,1:T(8,128)(2,1)S(1)} collective-permute-done((bf16[256,512]{0,1:T(8,128)(2,1)}, bf16[256,512]{0,1:T(8,128)(2,1)S(1)}, u32[]{:S(2)}, u32[]{:S(2)}) %collective-permute-start) | collective-permute-done | bytes 262176 | tf_op jit(solution)/shard_map/while/body/eval_jaxpr/ppermute | solution.py:15
  324.9 1.9 collective-permute-start
  327.0 13.3 %collective-permute-done = bf16[256,512]{0,1:T(8,128)(2,1)S(1)} collective-permute-done((bf16[256,512]{0,1:T(8,128)(2,1)}, bf16[256,512]{0,1:T(8,128)(2,1)S(1)}, u32[]{:S(2)}, u32[]{:S(2)}) %collective-permute-start) | collective-permute-done | bytes 262176 | tf_op jit(solution)/shard_map/while/body/eval_jaxpr/ppermute | solution.py:15
  343.2 1.9 collective-permute-start
  345.3 13.7 %collective-permute-done = bf16[256,512]{0,1:T(8,128)(2,1)S(1)} collective-permute-done((bf16[256,512]{0,1:T(8,128)(2,1)}, bf16[256,512]{0,1:T(8,128)(2,1)S(1)}, u32[]{:S(2)}, u32[]{:S(2)}) %collective-permute-start) | collective-permute-done | bytes 262176 | tf_op jit(solution)/shard_map/while/body/eval_jaxpr/ppermute | solution.py:15
  362.0 1.9 collective-permute-start
  364.1 13.7 %collective-permute-done = bf16[256,512]{0,1:T(8,128)(2,1)S(1)} collective-permute-done((bf16[256,512]{0,1:T(8,128)(2,1)}, bf16[256,512]{0,1:T(8,128)(2,1)S(1)}, u32[]{:S(2)}, u32[]{:S(2)}) %collective-permute-start) | collective-permute-done | bytes 262176 | tf_op jit(solution)/shard_map/while/body/eval_jaxpr/ppermute | solution.py:15
  380.7 1.9 collective-permute-start
  382.8 13.8 %collective-permute-done = bf16[256,512]{0,1:T(8,128)(2,1)S(1)} collective-permute-done((bf16[256,512]{0,1:T(8,128)(2,1)}, bf16[256,512]{0,1:T(8,128)(2,1)S(1)}, u32[]{:S(2)}, u32[]{:S(2)}) %collective-permute-start) | collective-permute-done | bytes 262176 | tf_op jit(solution)/shard_map/while/body/eval_jaxpr/ppermute | solution.py:15
  399.5 1.9 collective-permute-start
  401.6 13.6 %collective-permute-done = bf16[256,512]{0,1:T(8,128)(2,1)S(1)} collective-permute-done((bf16[256,512]{0,1:T(8,128)(2,1)}, bf16[256,512]{0,1:T(8,128)(2,1)S(1)}, u32[]{:S(2)}, u32[]{:S(2)}) %collective-permute-start) | collective-permute-done | bytes 262176 | tf_op jit(solution)/shard_map/while/body/eval_jaxpr/ppermute | solution.py:15
  420.2 13.7 %collective-permute-done = bf16[256,512]{0,1:T(8,128)(2,1)S(1)} collective-permute-done((bf16[256,512]{0,1:T(8,128)(2,1)}, bf16[256,512]{0,1:T(8,128)(2,1)S(1)}, u32[]{:S(2)}, u32[]{:S(2)}) %collective-permute-start) | collective-permute-done | bytes 262176 | tf_op jit(solution)/shard_map/while/body/eval_jaxpr/ppermute | solution.py:15
  436.9 1.9 collective-permute-start
  439.0 13.6 %collective-permute-done = bf16[256,512]{0,1:T(8,128)(2,1)S(1)} collective-permute-done((bf16[256,512]{0,1:T(8,128)(2,1)}, bf16[256,512]{0,1:T(8,128)(2,1)S(1)}, u32[]{:S(2)}, u32[]{:S(2)}) %collective-permute-start) | collective-permute-done | bytes 262176 | tf_op jit(solution)/shard_map/while/body/eval_jaxpr/ppermute | solution.py:15
  455.5 1.9 collective-permute-start
  457.6 13.3 %collective-permute-done = bf16[256,512]{0,1:T(8,128)(2,1)S(1)} collective-permute-done((bf16[256,512]{0,1:T(8,128)(2,1)}, bf16[256,512]{0,1:T(8,128)(2,1)S(1)}, u32[]{:S(2)}, u32[]{:S(2)}) %collective-permute-start) | collective-permute-done | bytes 262176 | tf_op jit(solution)/shard_map/while/body/eval_jaxpr/ppermute | solution.py:15
  476.0 13.3 %collective-permute-done = bf16[256,512]{0,1:T(8,128)(2,1)S(1)} collective-permute-done((bf16[256,512]{0,1:T(8,128)(2,1)}, bf16[256,512]{0,1:T(8,128)(2,1)S(1)}, u32[]{:S(2)}, u32[]{:S(2)}) %collective-permute-start) | collective-permute-done | bytes 262176 | tf_op jit(solution)/shard_map/while/body/eval_jaxpr/ppermute | solution.py:15
  494.3 13.3 %collective-permute-done = bf16[256,512]{0,1:T(8,128)(2,1)S(1)} collective-permute-done((bf16[256,512]{0,1:T(8,128)(2,1)}, bf16[256,512]{0,1:T(8,128)(2,1)S(1)}, u32[]{:S(2)}, u32[]{:S(2)}) %collective-permute-start) | collective-permute-done | bytes 262176 | tf_op jit(solution)/shard_map/while/body/eval_jaxpr/ppermute | solution.py:15
  510.6 1.9 collective-permute-start
  512.7 13.3 %collective-permute-done = bf16[256,512]{0,1:T(8,128)(2,1)S(1)} collective-permute-done((bf16[256,512]{0,1:T(8,128)(2,1)}, bf16[256,512]{0,1:T(8,128)(2,1)S(1)}, u32[]{:S(2)}, u32[]{:S(2)}) %collective-permute-start) | collective-permute-done | bytes 262176 | tf_op jit(solution)/shard_map/while/body/eval_jaxpr/ppermute | solution.py:15
  531.1 13.3 %collective-permute-done = bf16[256,512]{0,1:T(8,128)(2,1)S(1)} collective-permute-done((bf16[256,512]{0,1:T(8,128)(2,1)}, bf16[256,512]{0,1:T(8,128)(2,1)S(1)}, u32[]{:S(2)}, u32[]{:S(2)}) %collective-permute-start) | collective-permute-done | bytes 262176 | tf_op jit(solution)/shard_map/while/body/eval_jaxpr/ppermute | solution.py:15
  549.4 13.3 %collective-permute-done = bf16[256,512]{0,1:T(8,128)(2,1)S(1)} collective-permute-done((bf16[256,512]{0,1:T(8,128)(2,1)}, bf16[256,512]{0,1:T(8,128)(2,1)S(1)}, u32[]{:S(2)}, u32[]{:S(2)}) %collective-permute-start) | collective-permute-done | bytes 262176 | tf_op jit(solution)/shard_map/while/body/eval_jaxpr/ppermute | solution.py:15
  567.8 13.3 %collective-permute-done = bf16[256,512]{0,1:T(8,128)(2,1)S(1)} collective-permute-done((bf16[256,512]{0,1:T(8,128)(2,1)}, bf16[256,512]{0,1:T(8,128)(2,1)S(1)}, u32[]{:S(2)}, u32[]{:S(2)}) %collective-permute-start) | collective-permute-done | bytes 262176 | tf_op jit(solution)/shard_map/while/body/eval_jaxpr/ppermute | solution.py:15
  586.8 2.4 multiply_reduce_fusion
  590.6 380.1 %psum.7 = f32[4,1024]{1,0:T(4,128)S(1)} all-reduce(f32[4,1024]{1,0:T(4,128)S(1)} %broadcast_select_fusion.2), channel_id=1, replica_groups=mesh['dp'=8,'ctx'=64] {'ctx'}, use_global_device_ids=true, to_apply=%region_10.11 | all-reduce | flops 4096 | bytes 32768 | tf_op jit(solution)/shard_map/psum | solution.py:165
  974.4 8.4 while.34
  983.2 41.5 %all-reduce.2 = (f32[32]{0:T(128)S(1)}, f32[32]{0:T(128)S(1)}) all-reduce(f32[32]{0:T(128)S(1)} %dynamic-update-slice, f32[32]{0:T(128)S(1)} %dynamic-update-slice.1), channel_id=1, replica_groups=mesh['dp'=8,'ctx'=64] {'dp'}, use_global_device_ids=true, to_apply=%add | all-reduce | flops 64 | bytes 512
  (398 shorter events, 89.7 us)
Async XLA Ops:
  7.2 6.6 copy-start
  7.2 3.9 copy-start.15
  7.2 5.9 copy-start.4
  7.2 252.1 %all-gather.5.cloned.1.call-start = ((), (), s32[]{:S(2)}) async-start(), calls=%async_computation | async-start | bytes 1179648 | tf_op jit(solution)/shard_map/all_gather | solution.py:113
  7.9 254.1 %all-gather.7.cloned.1.call-start = ((), (), s32[]{:S(2)}) async-start(), calls=%async_computation.1 | async-start | bytes 2359296 | tf_op jit(solution)/shard_map/all_gather | solution.py:112
  8.7 578.1 %all-gather.9.cloned.1.call-start = ((), (), s32[]{:S(2)}) async-start(), calls=%async_computation.2 | async-start | bytes 2359296 | tf_op jit(solution)/shard_map/all_gather | solution.py:132
  9.4 962.3 %all-gather.11.cloned.1.call-start = ((), (), s32[]{:S(2)}) async-start(), calls=%async_computation.3 | async-start | bytes 2129920 | tf_op jit(solution)/shard_map/all_gather | solution.py:19
  11.0 248.3 %copy-start.1 = (bf16[256,1024]{1,0:T(8,128)(2,1)S(1)}, bf16[256,1024]{1,0:T(8,128)(2,1)}, u32[]{:S(2)}) copy-start(bf16[256,1024]{1,0:T(8,128)(2,1)} %param.17) | copy-start | bytes 1572868
  11.0 247.4 %copy-start.6 = (pred[4]{0:T(512)(128)(4,1)}, pred[4]{0:T(512)(128)(4,1)S(1)}, u32[]{:S(2)}) copy-start(pred[4]{0:T(512)(128)(4,1)S(1)} %iota_compare_fusion.2) | copy-start | bytes 16
  139.6 124.7 %copy-start.2 = (f32[64,4,16]{2,1,0:T(4,128)}, f32[64,4,16]{2,1,0:T(4,128)S(1)}, u32[]{:S(2)}) copy-start(f32[64,4,16]{2,1,0:T(4,128)S(1)} %all_gather.31) | copy-start | bytes 49156
  269.1 52.8 %collective-permute-start = (bf16[256,512]{0,1:T(8,128)(2,1)}, bf16[256,512]{0,1:T(8,128)(2,1)S(1)}, u32[]{:S(2)}, u32[]{:S(2)}) collective-permute-start(bf16[256,512]{0,1:T(8,128)(2,1)} %get-tuple-element.434), channel_id=1, source_target_pairs={{0,1},{1,2},{2,3},{3,4},{4,5},{5,6},{6,7},{7,8},{8,9},{9,10},{10,1... | collective-permute-start | bytes 786440 | tf_op jit(solution)/shard_map/while/body/eval_jaxpr/ppermute | solution.py:15
  324.9 15.4 %collective-permute-start = (bf16[256,512]{0,1:T(8,128)(2,1)}, bf16[256,512]{0,1:T(8,128)(2,1)S(1)}, u32[]{:S(2)}, u32[]{:S(2)}) collective-permute-start(bf16[256,512]{0,1:T(8,128)(2,1)} %get-tuple-element.434), channel_id=1, source_target_pairs={{0,1},{1,2},{2,3},{3,4},{4,5},{5,6},{6,7},{7,8},{8,9},{9,10},{10,1... | collective-permute-start | bytes 786440 | tf_op jit(solution)/shard_map/while/body/eval_jaxpr/ppermute | solution.py:15
  343.2 15.8 %collective-permute-start = (bf16[256,512]{0,1:T(8,128)(2,1)}, bf16[256,512]{0,1:T(8,128)(2,1)S(1)}, u32[]{:S(2)}, u32[]{:S(2)}) collective-permute-start(bf16[256,512]{0,1:T(8,128)(2,1)} %get-tuple-element.434), channel_id=1, source_target_pairs={{0,1},{1,2},{2,3},{3,4},{4,5},{5,6},{6,7},{7,8},{8,9},{9,10},{10,1... | collective-permute-start | bytes 786440 | tf_op jit(solution)/shard_map/while/body/eval_jaxpr/ppermute | solution.py:15
  362.0 15.7 %collective-permute-start = (bf16[256,512]{0,1:T(8,128)(2,1)}, bf16[256,512]{0,1:T(8,128)(2,1)S(1)}, u32[]{:S(2)}, u32[]{:S(2)}) collective-permute-start(bf16[256,512]{0,1:T(8,128)(2,1)} %get-tuple-element.434), channel_id=1, source_target_pairs={{0,1},{1,2},{2,3},{3,4},{4,5},{5,6},{6,7},{7,8},{8,9},{9,10},{10,1... | collective-permute-start | bytes 786440 | tf_op jit(solution)/shard_map/while/body/eval_jaxpr/ppermute | solution.py:15
  380.7 15.9 %collective-permute-start = (bf16[256,512]{0,1:T(8,128)(2,1)}, bf16[256,512]{0,1:T(8,128)(2,1)S(1)}, u32[]{:S(2)}, u32[]{:S(2)}) collective-permute-start(bf16[256,512]{0,1:T(8,128)(2,1)} %get-tuple-element.434), channel_id=1, source_target_pairs={{0,1},{1,2},{2,3},{3,4},{4,5},{5,6},{6,7},{7,8},{8,9},{9,10},{10,1... | collective-permute-start | bytes 786440 | tf_op jit(solution)/shard_map/while/body/eval_jaxpr/ppermute | solution.py:15
  399.5 15.7 %collective-permute-start = (bf16[256,512]{0,1:T(8,128)(2,1)}, bf16[256,512]{0,1:T(8,128)(2,1)S(1)}, u32[]{:S(2)}, u32[]{:S(2)}) collective-permute-start(bf16[256,512]{0,1:T(8,128)(2,1)} %get-tuple-element.434), channel_id=1, source_target_pairs={{0,1},{1,2},{2,3},{3,4},{4,5},{5,6},{6,7},{7,8},{8,9},{9,10},{10,1... | collective-permute-start | bytes 786440 | tf_op jit(solution)/shard_map/while/body/eval_jaxpr/ppermute | solution.py:15
  418.2 15.8 %collective-permute-start = (bf16[256,512]{0,1:T(8,128)(2,1)}, bf16[256,512]{0,1:T(8,128)(2,1)S(1)}, u32[]{:S(2)}, u32[]{:S(2)}) collective-permute-start(bf16[256,512]{0,1:T(8,128)(2,1)} %get-tuple-element.434), channel_id=1, source_target_pairs={{0,1},{1,2},{2,3},{3,4},{4,5},{5,6},{6,7},{7,8},{8,9},{9,10},{10,1... | collective-permute-start | bytes 786440 | tf_op jit(solution)/shard_map/while/body/eval_jaxpr/ppermute | solution.py:15
  436.9 15.7 %collective-permute-start = (bf16[256,512]{0,1:T(8,128)(2,1)}, bf16[256,512]{0,1:T(8,128)(2,1)S(1)}, u32[]{:S(2)}, u32[]{:S(2)}) collective-permute-start(bf16[256,512]{0,1:T(8,128)(2,1)} %get-tuple-element.434), channel_id=1, source_target_pairs={{0,1},{1,2},{2,3},{3,4},{4,5},{5,6},{6,7},{7,8},{8,9},{9,10},{10,1... | collective-permute-start | bytes 786440 | tf_op jit(solution)/shard_map/while/body/eval_jaxpr/ppermute | solution.py:15
  455.5 15.4 %collective-permute-start = (bf16[256,512]{0,1:T(8,128)(2,1)}, bf16[256,512]{0,1:T(8,128)(2,1)S(1)}, u32[]{:S(2)}, u32[]{:S(2)}) collective-permute-start(bf16[256,512]{0,1:T(8,128)(2,1)} %get-tuple-element.434), channel_id=1, source_target_pairs={{0,1},{1,2},{2,3},{3,4},{4,5},{5,6},{6,7},{7,8},{8,9},{9,10},{10,1... | collective-permute-start | bytes 786440 | tf_op jit(solution)/shard_map/while/body/eval_jaxpr/ppermute | solution.py:15
  473.9 15.4 %collective-permute-start = (bf16[256,512]{0,1:T(8,128)(2,1)}, bf16[256,512]{0,1:T(8,128)(2,1)S(1)}, u32[]{:S(2)}, u32[]{:S(2)}) collective-permute-start(bf16[256,512]{0,1:T(8,128)(2,1)} %get-tuple-element.434), channel_id=1, source_target_pairs={{0,1},{1,2},{2,3},{3,4},{4,5},{5,6},{6,7},{7,8},{8,9},{9,10},{10,1... | collective-permute-start | bytes 786440 | tf_op jit(solution)/shard_map/while/body/eval_jaxpr/ppermute | solution.py:15
  492.2 15.4 %collective-permute-start = (bf16[256,512]{0,1:T(8,128)(2,1)}, bf16[256,512]{0,1:T(8,128)(2,1)S(1)}, u32[]{:S(2)}, u32[]{:S(2)}) collective-permute-start(bf16[256,512]{0,1:T(8,128)(2,1)} %get-tuple-element.434), channel_id=1, source_target_pairs={{0,1},{1,2},{2,3},{3,4},{4,5},{5,6},{6,7},{7,8},{8,9},{9,10},{10,1... | collective-permute-start | bytes 786440 | tf_op jit(solution)/shard_map/while/body/eval_jaxpr/ppermute | solution.py:15
  510.6 15.4 %collective-permute-start = (bf16[256,512]{0,1:T(8,128)(2,1)}, bf16[256,512]{0,1:T(8,128)(2,1)S(1)}, u32[]{:S(2)}, u32[]{:S(2)}) collective-permute-start(bf16[256,512]{0,1:T(8,128)(2,1)} %get-tuple-element.434), channel_id=1, source_target_pairs={{0,1},{1,2},{2,3},{3,4},{4,5},{5,6},{6,7},{7,8},{8,9},{9,10},{10,1... | collective-permute-start | bytes 786440 | tf_op jit(solution)/shard_map/while/body/eval_jaxpr/ppermute | solution.py:15
  529.0 15.4 %collective-permute-start = (bf16[256,512]{0,1:T(8,128)(2,1)}, bf16[256,512]{0,1:T(8,128)(2,1)S(1)}, u32[]{:S(2)}, u32[]{:S(2)}) collective-permute-start(bf16[256,512]{0,1:T(8,128)(2,1)} %get-tuple-element.434), channel_id=1, source_target_pairs={{0,1},{1,2},{2,3},{3,4},{4,5},{5,6},{6,7},{7,8},{8,9},{9,10},{10,1... | collective-permute-start | bytes 786440 | tf_op jit(solution)/shard_map/while/body/eval_jaxpr/ppermute | solution.py:15
  547.4 15.4 %collective-permute-start = (bf16[256,512]{0,1:T(8,128)(2,1)}, bf16[256,512]{0,1:T(8,128)(2,1)S(1)}, u32[]{:S(2)}, u32[]{:S(2)}) collective-permute-start(bf16[256,512]{0,1:T(8,128)(2,1)} %get-tuple-element.434), channel_id=1, source_target_pairs={{0,1},{1,2},{2,3},{3,4},{4,5},{5,6},{6,7},{7,8},{8,9},{9,10},{10,1... | collective-permute-start | bytes 786440 | tf_op jit(solution)/shard_map/while/body/eval_jaxpr/ppermute | solution.py:15
  565.7 15.4 %collective-permute-start = (bf16[256,512]{0,1:T(8,128)(2,1)}, bf16[256,512]{0,1:T(8,128)(2,1)S(1)}, u32[]{:S(2)}, u32[]{:S(2)}) collective-permute-start(bf16[256,512]{0,1:T(8,128)(2,1)} %get-tuple-element.434), channel_id=1, source_target_pairs={{0,1},{1,2},{2,3},{3,4},{4,5},{5,6},{6,7},{7,8},{8,9},{9,10},{10,1... | collective-permute-start | bytes 786440 | tf_op jit(solution)/shard_map/while/body/eval_jaxpr/ppermute | solution.py:15
  589.2 381.5 %copy-start.12 = (f32[1024]{0:T(1024)S(1)}, f32[1024]{0:T(1024)}, u32[]{:S(2)}) copy-start(f32[1024]{0:T(1024)} %param.22) | copy-start | bytes 12292
  589.2 381.4 %copy-start.13 = (f32[4]{0:T(128)S(1)}, f32[4]{0:T(128)}, u32[]{:S(2)}) copy-start(f32[4]{0:T(128)} %get-tuple-element.297) | copy-start | bytes 52
  971.7 2.7 slice-start.1
  971.7 11.1 %copy-start.5 = (f32[2048]{0:T(1024)S(1)}, f32[2048]{0:T(1024)}, u32[]{:S(2)}) copy-start(f32[2048]{0:T(1024)} %param.26) | copy-start | bytes 24580
  971.7 53.1 %copy-start.16 = (s32[32]{0:T(128)S(1)}, s32[32]{0:T(128)}, u32[]{:S(2)}) copy-start(s32[32]{0:T(128)} %param.29) | copy-start | bytes 388
  971.7 53.1 %copy-start.10 = (s32[32]{0:T(128)S(1)}, s32[32]{0:T(128)}, u32[]{:S(2)}) copy-start(s32[32]{0:T(128)} %param.28) | copy-start | bytes 388
  983.0 42.9 %copy-start.14 = (f32[4]{0:T(128)}, f32[4]{0:T(128)S(1)}, u32[]{:S(2)}) copy-start(f32[4]{0:T(128)S(1)} %multiply_reduce_fusion.1) | copy-start | bytes 52
  (6 other events, 11.7 us)
Sparse Core Ops, SparseCore 0:
  11.2 95.8 all-gather.4
  110.3 111.1 all-gather.6
  224.7 112.8 all-gather.8
  339.6 114.5 all-gather.10
where the time goes:
time: 1030 us
  blocking collectives  664 us (64%)
  waiting for transfers between devices  241 us (23%)
  matrix products  33.6 us (3%)
  starting transfers between devices  29.1 us (3%)
  other arithmetic  25.9 us (3%)
  local copies, waits for them, and re-layouts  21.2 us (2%)
  between operations  14.9 us (1%)
    psum x1, blocking collectives, local(): pool_all = lax.psum(pool_slots, 'ctx')  380 us
    all_gather x2, blocking collectives, joined(): pieces = jax.tree.map(lambda part: lax.all_gather(part, axis), value)  242 us
    ppermute x15, waiting for transfers between devices, shifted_2(): lax.ppermute(value, axis, [(source, source + steps) for source in range(f...  239 us
    unnamed x1, blocking collectives  41.5 us
    ppermute x15, starting transfers between devices, shifted_2(): lax.ppermute(value, axis, [(source, source + steps) for source in range(f...  29 us
  transfers between devices with their start and end apart: 19, of which 15 were waited for; matrix products, arithmetic and copies ran while one was open for 7% of the time, Pallas kernels for 0%

commit v1 on v0

v1 whole, which is shorter than its diff:
```python
import functools

import jax
import jax.numpy as jnp
from jax import lax
from jax.experimental import pallas as pl
from jax.experimental.pallas import tpu as pltpu
from jax.sharding import PartitionSpec as P

HEADS = 8
KV_HEADS = 2
GROUPS = 4
HD = 128
T_HEADS = 16
ROWS = 256
D = 1024
CHIPS = 8
BIG = -1e30
F32 = jnp.float32
BF16 = jnp.bfloat16
SCALE = HD ** (-0.5)
LOG2E = 1.4426950408889634
MESH = pl.DeviceIdType.MESH


def kernel(
    hid_in, wkv_in, wq_in, wo_in, gain_in, shead_in, tq_in, tk_in, tv_in, thead_in, len_in, list_in, rel_in,
    out_ref, pooled_ref, tscore_ref, div_ref,
    hid, wkv, wq, wo, tk, tv, kvb, relay, qt, att, m_ref, l_ref, acc_ref,
    tbuf, chain, cstage, pbuf, ybuf, dbuf,
    gain_ref, shead_ref, tq_ref, thead_ref, len_ref, list_ref, rel_ref,
    lsem, wsend, wrecv, kv_recv, kv_send, sib_send, rev_send, relay_recv, relay_send,
    t_send, t_recv, c_send, c_recv, p_send, p_recv, y_send, y_recv, d_send, d_recv,
):
    dp = lax.axis_index("dp")
    ctx = lax.axis_index("ctx")
    x, zh = dp // 2, dp % 2
    y, pos = ctx // 16, ctx % 16
    c, k = pos // 2, pos % 2
    oz = 1 - zh
    other_dp = 2 * x + oz
    sib_ctx = ctx + 1 - 2 * k
    line = y * 16

    def remote(src, dst, ssem, rsem, to_dp, to_ctx):
        return pltpu.make_async_remote_copy(
            src_ref=src, dst_ref=dst, send_sem=ssem, recv_sem=rsem, device_id=(to_dp, to_ctx), device_id_type=MESH
        )

    def x_peer(d):
        return 2 * ((x + d) % 4) + zh

    def y_peer(d):
        return ((y + d) % 4) * 16 + pos

    lane = 64 * k
    locals_ = [
        pltpu.make_async_copy(hid_in, hid, lsem.at[0]),
        pltpu.make_async_copy(tk_in, tk, lsem.at[1]),
        pltpu.make_async_copy(tv_in, tv, lsem.at[2]),
    ]
    weights = [(wkv_in, wkv), (wq_in, wq), (wo_in, wo)]
    for i, (w_in, w) in enumerate(weights):
        locals_.append(
            pltpu.make_async_copy(w_in.at[pl.ds(lane, 64)], w.at[x, zh, pl.ds(lane, 64)], lsem.at[3 + i])
        )
    small = [
        (gain_in, gain_ref), (shead_in, shead_ref), (tq_in, tq_ref), (thead_in, thead_ref), (len_in, len_ref),
        (list_in, list_ref), (rel_in, rel_ref),
    ]
    small = [pltpu.make_async_copy(src, dst, lsem.at[6 + i]) for i, (src, dst) in enumerate(small)]
    for copy in (locals_[0], locals_[3], locals_[1], locals_[2], locals_[4], locals_[5]):
        copy.start()
    for copy in small:
        copy.start()

    barrier = pltpu.get_barrier_semaphore()

    def greet(to_dp, to_ctx):
        pl.semaphore_signal(barrier, inc=1, device_id=(to_dp, to_ctx), device_id_type=MESH)

    for d in range(1, 16):
        greet(dp, line + (pos + d) % 16)
    for d in range(1, 4):
        greet(dp, y_peer(d))
    for d in range(1, 8):
        greet((dp + d) % 8, ctx)

    @pl.when(c == 0)
    def _():
        for j in range(4, 8):
            greet(other_dp, line + 2 * j + k)

    @pl.when(c == 7)
    def _():
        for j in range(4):
            greet(other_dp, line + 2 * j + k)

    @pl.when(jnp.logical_and(c >= 1, c <= 3))
    def _():
        greet(other_dp, line + 14 + k)

    @pl.when(jnp.logical_and(c >= 4, c <= 6))
    def _():
        greet(other_dp, line + k)

    pl.semaphore_wait(barrier, 26 + 3 * (c // 7 + 1 - (c + 6) // 7))

    class Gather:
        def __init__(self, i):
            self.i = i
            self.w_in, self.w = weights[i]
            self.piece = 64 * k + 16 * y

        def sem(self, table, n):
            return table.at[self.i, n]

        def z_copy(self, j):
            w = self.w.at[x, zh, pl.ds(self.piece, 16)]
            return remote(
                self.w_in.at[pl.ds(self.piece, 16)], w, self.sem(wsend, j % 4), self.sem(wrecv, 0),
                other_dp, line + 2 * j + k,
            )

        def z_start(self):
            @pl.when(c == 0)
            def _():
                for j in range(4, 8):
                    self.z_copy(j).start()

            @pl.when(c == 7)
            def _():
                for j in range(4):
                    self.z_copy(j).start()

        def z_recv(self):
            w = self.w.at[x, oz, pl.ds(self.piece, 16)]
            remote(w, w, self.sem(wsend, 0), self.sem(wrecv, 0), other_dp, ctx).wait_recv()

        def own_copy(self, d):
            return remote(
                self.w_in.at[pl.ds(lane, 64)], self.w.at[x, zh, pl.ds(lane, 64)],
                self.sem(wsend, 3 + d), self.sem(wrecv, d), x_peer(d), ctx,
            )

        def own_start(self):
            for d in range(1, 4):
                self.own_copy(d).start()

        def own_recv(self):
            for d in range(1, 4):
                w = self.w.at[(x + 4 - d) % 4, zh, pl.ds(lane, 64)]
                remote(w, w, self.sem(wsend, 0), self.sem(wrecv, d), dp, ctx).wait_recv()

        def other_copy(self, d):
            w = self.w.at[x, oz, pl.ds(self.piece, 16)]
            return remote(w, w, self.sem(wsend, 6 + d), self.sem(wrecv, 3 + d), x_peer(d), ctx)

        def other_start(self):
            for d in range(1, 4):
                self.other_copy(d).start()

        def other_recv(self):
            for d in range(1, 4):
                w = self.w.at[(x + 4 - d) % 4, oz, pl.ds(self.piece, 16)]
                remote(w, w, self.sem(wsend, 0), self.sem(wrecv, 3 + d), dp, ctx).wait_recv()

        def y_copy(self, d):
            w = self.w.at[:, oz, pl.ds(self.piece, 16)]
            return remote(w, w, self.sem(wsend, 9 + d), self.sem(wrecv, 6 + d), dp, y_peer(d))

        def y_start(self):
            for d in range(1, 4):
                self.y_copy(d).start()

        def y_recv(self):
            for d in range(1, 4):
                w = self.w.at[:, oz, pl.ds(64 * k + 16 * ((y + 4 - d) % 4), 16)]
                remote(w, w, self.sem(wsend, 0), self.sem(wrecv, 6 + d), dp, ctx).wait_recv()

        def sib_copy(self, half, n):
            w = self.w.at[:, half, pl.ds(lane, 64)]
            return remote(w, w, self.sem(wsend, 13 + n), self.sem(wrecv, 10 + n), dp, sib_ctx)

        def sib_recv(self, half, n):
            w = self.w.at[:, half, pl.ds(64 - lane, 64)]
            remote(w, w, self.sem(wsend, 0), self.sem(wrecv, 10 + n), dp, ctx).wait_recv()

        def finish(self):
            @pl.when(c == 0)
            def _():
                for j in range(4, 8):
                    self.z_copy(j).wait_send()

            @pl.when(c == 7)
            def _():
                for j in range(4):
                    self.z_copy(j).wait_send()

            for d in range(1, 4):
                self.own_copy(d).wait_send()
                self.other_copy(d).wait_send()
                self.y_copy(d).wait_send()
            self.sib_copy(zh, 0).wait_send()
            self.sib_copy(oz, 1).wait_send()

    gkv, gq, go = Gather(0), Gather(1), Gather(2)
    gkv.z_start()
    gkv.own_start()
    gkv.z_recv()
    gkv.other_start()
    gkv.own_recv()
    locals_[3].wait()
    gkv.sib_copy(zh, 0).start()
    gkv.other_recv()
    gkv.y_start()
    gq.z_start()
    gq.own_start()

    locals_[0].wait()

    def hid_half(half):
        parts = [hid[:, pl.ds(pl.multiple_of((2 * i + half) * 128, 128), 128)] for i in range(4)]
        return jnp.concatenate(parts, axis=1)

    gkv.sib_recv(zh, 0)
    kv_own = jnp.dot(hid_half(zh), wkv[:, zh].reshape(512, 512), preferred_element_type=F32)
    acc_ref[0:4] = jnp.concatenate([kv_own[:, :256], kv_own[:, 256:]], axis=0).reshape(4, 128, 256)

    gkv.y_recv()
    gkv.sib_copy(oz, 1).start()

    for copy in small:
        copy.wait()
    length = len_ref[dp * 4 + y]
    locals_[1].wait()
    locals_[2].wait()
    slot_row = lax.broadcasted_iota(jnp.int32, (4, 2048), 0) == y
    own_q = jnp.sum(jnp.where(slot_row, tq_ref[...].astype(F32), 0.0), axis=0, keepdims=True)
    head_of = lax.broadcasted_iota(jnp.int32, (T_HEADS, 2048), 1) // HD
    diagonal = head_of == lax.broadcasted_iota(jnp.int32, (T_HEADS, 2048), 0)
    q_heads = jnp.where(diagonal, own_q, 0.0).astype(BF16)
    ts = lax.dot_general(q_heads, tk[...], (((1,), (1,)), ((), ())), preferred_element_type=F32) * SCALE
    t_valid = pos * ROWS + lax.broadcasted_iota(jnp.int32, (T_HEADS, ROWS), 1) < length
    ts = jnp.where(t_valid, ts, BIG)
    t_best = jnp.max(ts, axis=1, keepdims=True)
    t_weights = jnp.where(t_valid, jnp.exp(ts - t_best), 0.0)
    t_total = jnp.sum(t_weights, axis=1, keepdims=True)
    t_out = jnp.dot(t_weights.astype(BF16), tv[...], preferred_element_type=F32)
    t_sum = jnp.sum(jnp.where(diagonal, t_out * thead_ref[...], 0.0), axis=1, keepdims=True)
    eye = lax.broadcasted_iota(jnp.int32, (T_HEADS, 128), 0) == lax.broadcasted_iota(jnp.int32, (T_HEADS, 128), 1)

    def row_of(column):
        return jnp.sum(jnp.where(eye, column, 0.0), axis=0, keepdims=True)

    tbuf[pos] = jnp.concatenate([row_of(t_best), row_of(t_total), row_of(t_sum)], axis=1)

    def t_copy(d):
        return remote(tbuf.at[pos], tbuf.at[pos], t_send.at[d], t_recv.at[d], dp, line + (pos + d) % 16)

    for d in range(1, 16):
        t_copy(d).start()

    gkv.sib_recv(oz, 1)
    kv_all = jnp.dot(hid_half(oz), wkv[:, oz].reshape(512, 512), preferred_element_type=F32)
    kv_first = acc_ref[0:4].reshape(512, 256)
    keys = (kv_all[:, :256] + kv_first[:256]).astype(BF16)
    own = 2 * c + k
    for h in range(KV_HEADS):
        kvb[own, 0, h] = keys[:, h * HD : (h + 1) * HD]

    def ring_copy(b, j):
        ref = kvb.at[2 * b + k, j]
        return remote(ref, ref, kv_send.at[b, j], kv_recv.at[2 * b + k, j], dp, ctx + 2)

    def back_copy(b, j):
        ref = kvb.at[2 * b + k, j]
        return remote(ref, ref, kv_send.at[b, j], kv_recv.at[2 * b + k, j], dp, ctx - 2)

    def sib_copy(b, j):
        ref = kvb.at[2 * b + k, j]
        return remote(ref, ref, sib_send.at[b, j], kv_recv.at[2 * b + k, j], dp, sib_ctx)

    def kv_wait(block, j):
        ref = kvb.at[block, j]
        remote(ref, ref, kv_send.at[0, 0], kv_recv.at[block, j], dp, ctx).wait_recv()

    def send_own(j):
        @pl.when(c < 7)
        def _():
            ring_copy(c, j).start()

        sib_copy(c, j).start()

    send_own(0)
    values = (kv_all[:, 256:] + kv_first[256:]).astype(BF16)
    for h in range(KV_HEADS):
        for part in range(2):
            block = values[part * 128 : (part + 1) * 128, h * HD : (h + 1) * HD]
            kvb[own, 1, h, pl.ds(part * 128, 128)] = block.T
    send_own(1)

    gq.z_recv()
    gq.other_start()
    gq.own_recv()
    locals_[4].wait()
    gq.sib_copy(zh, 0).start()
    go.z_start()
    go.own_start()
    gq.other_recv()
    gq.y_start()

    def attend(b, diag):
        for h in range(KV_HEADS):
            kp = jnp.concatenate([kvb[2 * b, 0, h], kvb[2 * b + 1, 0, h]], axis=0)
            v0, v1 = kvb[2 * b, 1, h], kvb[2 * b + 1, 1, h]
            vt = jnp.concatenate([v0[:128], v0[128:], v1[:128], v1[128:]], axis=1)
            for g in range(GROUPS):
                i = h * GROUPS + g
                s = jnp.dot(kp, qt[h, :, g * ROWS : (g + 1) * ROWS], preferred_element_type=F32) * (SCALE * LOG2E)
                if diag:
                    key = lax.broadcasted_iota(jnp.int32, (2 * ROWS, ROWS), 0)
                    row = lax.broadcasted_iota(jnp.int32, (2 * ROWS, ROWS), 1)
                    s = jnp.where(key <= k * ROWS + row, s, BIG)
                best = jnp.max(s, axis=0, keepdims=True)
                if not diag:
                    old = m_ref[i : i + 1, :]
                    best = jnp.maximum(old, best)
                    carry = jnp.exp2(old - best)
                p = jnp.exp2(s - best)
                total = jnp.sum(p, axis=0, keepdims=True)
                out = jnp.dot(vt, p.astype(BF16), preferred_element_type=F32)
                m_ref[i : i + 1, :] = best
                if diag:
                    l_ref[i : i + 1, :] = total
                    acc_ref[i] = out
                else:
                    l_ref[i : i + 1, :] = l_ref[i : i + 1, :] * carry + total
                    acc_ref[i] = acc_ref[i] * carry + out

    def forward(b):
        for j in range(2):
            kv_wait(2 * b + k, j)

            @pl.when(c < 7)
            def _():
                ring_copy(b, j).start()

            sib_copy(b, j).start()

    @pl.when(c >= 1)
    def _():
        forward(c - 1)

    gq.y_recv()
    gq.sib_copy(oz, 1).start()
    go.z_recv()
    go.other_start()
    gq.sib_recv(zh, 0)
    gq.sib_recv(oz, 1)
    query = jnp.dot(hid[...], wq[...].reshape(D, HEADS * HD), preferred_element_type=F32).astype(BF16)
    for i in range(HEADS):
        qt[i // GROUPS, :, (i % GROUPS) * ROWS : (i % GROUPS + 1) * ROWS] = query[:, i * HD : (i + 1) * HD].T
    go.own_recv()
    locals_[5].wait()
    go.sib_copy(zh, 0).start()
    for j in range(2):
        kv_wait(2 * c + 1 - k, j)
    attend(c, True)
    go.other_recv()
    go.y_start()

    def step(s, carry):
        @pl.when(s <= c)
        def _():
            forward(c - s)

        @pl.when(s == 2)
        def _():
            go.y_recv()
            go.sib_copy(oz, 1).start()

        @pl.when(s - 1 <= c)
        def _():
            b = c - s + 1
            for j in range(2):
                kv_wait(2 * b + 1 - k, j)
            attend(b, False)

        return carry

    lax.fori_loop(2, 9, step, 0)

    for i in range(HEADS):
        att[:, i * HD : (i + 1) * HD] = (acc_ref[i] / l_ref[i : i + 1, :]).astype(BF16).T
    go.sib_recv(zh, 0)
    go.sib_recv(oz, 1)
    hidden = hid[...].astype(F32) + jnp.dot(att[...], wo[...].reshape(D, D), preferred_element_type=F32)
    valid = pos * ROWS + lax.broadcasted_iota(jnp.int32, (ROWS, 1), 0) < length
    rate = jnp.where(valid, lax.rsqrt(jnp.mean(hidden * hidden, axis=1, keepdims=True) + 1e-05), 0.0)
    part = jnp.sum(hidden * rate, axis=0, keepdims=True) * gain_ref[...]
    out_ref[...] = jnp.where(valid, hidden, 0.0)

    def chain_copy():
        return remote(cstage, chain, c_send, c_recv, dp, ctx + 2)

    @pl.when(c == 0)
    def _():
        chain[...] = jnp.zeros_like(chain)

    @pl.when(jnp.logical_and(c >= 1, c <= 6))
    def _():
        remote(chain, chain, c_send, c_recv, dp, ctx).wait_recv()

    @pl.when(c <= 5)
    def _():
        cstage[...] = part + chain[...]
        chain_copy().start()

    def p_copy(r, d):
        return remote(pbuf.at[r], pbuf.at[r], p_send.at[d], p_recv.at[r], dp, line + (pos + d) % 16)

    root = 2 * (c - 6) + k

    @pl.when(c == 6)
    def _():
        pbuf[root] = part + chain[...]

    @pl.when(c == 7)
    def _():
        pbuf[root] = part

    @pl.when(c >= 6)
    def _():
        for d in range(1, 16):
            p_copy(root, d).start()

    for d in range(1, 16):
        ref = tbuf.at[(pos + 16 - d) % 16]
        remote(ref, ref, t_send.at[0], t_recv.at[d], dp, ctx).wait_recv()
    stats = jnp.concatenate([tbuf[i] for i in range(16)], axis=0)
    bests = stats[:, :128]
    factor = jnp.exp(bests - jnp.max(bests, axis=0, keepdims=True))
    total = jnp.sum(stats[:, 128:256] * factor, axis=0, keepdims=True)
    above = jnp.sum(stats[:, 256:] * factor, axis=0, keepdims=True)
    in_heads = lax.broadcasted_iota(jnp.int32, (1, 128), 1) < T_HEADS
    t_score = jnp.sum(jnp.where(in_heads, above / jnp.where(in_heads, total, 1.0), 0.0), axis=1, keepdims=True)

    for r in range(4):
        @pl.when(pos != 12 + r)
        def _():
            ref = pbuf.at[r]
            remote(ref, ref, c_send, p_recv.at[r], dp, ctx).wait_recv()

    pooled_sum = (pbuf[0] + pbuf[1]) + (pbuf[2] + pbuf[3])
    pooled = pooled_sum / length.astype(F32)
    ybuf[y] = jnp.concatenate([pooled, jnp.broadcast_to(t_score, (1, 128))], axis=1)

    def y_copy(d):
        return remote(ybuf.at[y], ybuf.at[y], y_send.at[d], y_recv.at[d], dp, y_peer(d))

    for d in range(1, 4):
        y_copy(d).start()
    for d in range(1, 4):
        ref = ybuf.at[(y + 4 - d) % 4]
        remote(ref, ref, y_send.at[0], y_recv.at[d], dp, ctx).wait_recv()

    lanes = lax.broadcasted_iota(jnp.int32, (1, 128), 1)
    scores = jnp.zeros((1, 128), F32)
    t_row = jnp.zeros((1, 128), F32)
    for i in range(4):
        row = ybuf[i]
        student = jnp.sum(row[:, :D] * shead_ref[...], axis=1, keepdims=True)
        scores = scores + jnp.where(lanes == dp * 4 + i, student, 0.0)
        scores = scores + jnp.where(lanes == 64 + dp * 4 + i, row[:, D:], 0.0)
        t_row = t_row + jnp.where(lanes == i, row[:, D:], 0.0)
        pooled_ref[i : i + 1, :] = row[:, :D]
    tscore_ref[...] = t_row
    dbuf[dp] = scores

    def d_copy(d):
        return remote(dbuf.at[dp], dbuf.at[dp], d_send.at[d], d_recv.at[d], (dp + d) % 8, ctx)

    for d in range(1, 8):
        d_copy(d).start()

    @pl.when(c < 7)
    def _():
        def sent(s, carry):
            for j in range(2):
                ring_copy(s, j).wait_send()
            return carry

        lax.fori_loop(0, c + 1, sent, 0)

    def sib_sent(s, carry):
        for j in range(2):
            sib_copy(s, j).wait_send()
        return carry

    lax.fori_loop(0, c + 1, sib_sent, 0)
    for gather in (gkv, gq, go):
        gather.finish()
    for d in range(1, 16):
        t_copy(d).wait_send()

    @pl.when(c <= 5)
    def _():
        chain_copy().wait_send()

    @pl.when(c >= 6)
    def _():
        for d in range(1, 16):
            p_copy(root, d).wait_send()

    for d in range(1, 4):
        y_copy(d).wait_send()

    for d in range(1, 8):
        ref = dbuf.at[(dp + 8 - d) % 8]
        remote(ref, ref, d_send.at[0], d_recv.at[d], dp, ctx).wait_recv()
    every = dbuf[0]
    for i in range(1, 8):
        every = every + dbuf[i]

    threads = list_ref.shape[1]
    student_all, teacher_all = every[:, :threads], every[:, 64 : 64 + threads]
    target = teacher_all + rel_ref[...].astype(F32)
    member = lax.broadcasted_iota(jnp.int32, (8, threads), 0) == list_ref[...]

    def log_soft(logits):
        masked = jnp.where(member, logits, BIG)
        top = jnp.max(masked, axis=1, keepdims=True)
        shifted = jnp.where(member, jnp.exp(masked - top), 0.0)
        return masked - top - jnp.log(jnp.sum(shifted, axis=1, keepdims=True))

    target_log = log_soft(target)
    student_log = log_soft(student_all)
    target_prob = jnp.where(member, jnp.exp(target_log), 0.0)
    terms = jnp.where(member, target_prob * (target_log - student_log), 0.0)
    div_ref[...] = jnp.broadcast_to(jnp.sum(terms, axis=1, keepdims=True), (8, 128))

    for d in range(1, 8):
        d_copy(d).wait_send()


def local(
    student_hidden, w_query, w_keyval, w_out, norm_gain, student_head, teacher_query, teacher_keys, teacher_values,
    teacher_head, thread_lengths, list_index, relevance,
):
    vmem = pl.BlockSpec(memory_space=pltpu.VMEM)
    anywhere = pl.BlockSpec(memory_space=pl.ANY)
    dma = pltpu.SemaphoreType.DMA
    out, pooled, tscore, div = pl.pallas_call(
        kernel,
        out_shape=(
            jax.ShapeDtypeStruct((ROWS, D), F32),
            jax.ShapeDtypeStruct((4, D), F32),
            jax.ShapeDtypeStruct((1, 128), F32),
            jax.ShapeDtypeStruct((8, 128), F32),
        ),
        in_specs=[anywhere] * 13,
        out_specs=(vmem,) * 4,
        scratch_shapes=[
            pltpu.VMEM((ROWS, D), BF16),
            pltpu.VMEM((4, 2, 128, 512), BF16),
            pltpu.VMEM((4, 2, 128, D), BF16),
            pltpu.VMEM((4, 2, 128, D), BF16),
            pltpu.VMEM((ROWS, 2048), BF16),
            pltpu.VMEM((ROWS, 2048), BF16),
            pltpu.VMEM((16, 2, KV_HEADS, 256, 128), BF16),
            pltpu.VMEM((2, 2, KV_HEADS, 256, 128), BF16),
            pltpu.VMEM((KV_HEADS, HD, GROUPS * ROWS), BF16),
            pltpu.VMEM((ROWS, D), BF16),
            pltpu.VMEM((HEADS, ROWS), F32),
            pltpu.VMEM((HEADS, ROWS), F32),
            pltpu.VMEM((HEADS, HD, ROWS), F32),
            pltpu.VMEM((16, 1, 384), F32),
            pltpu.VMEM((1, D), F32),
            pltpu.VMEM((1, D), F32),
            pltpu.VMEM((4, 1, D), F32),
            pltpu.VMEM((4, 1, D + 128), F32),
            pltpu.VMEM((8, 1, 128), F32),
            pltpu.VMEM((1, D), F32),
            pltpu.VMEM((1, D), F32),
            pltpu.VMEM((4, 2048), BF16),
            pltpu.VMEM((1, 2048), F32),
            pltpu.SMEM((32,), jnp.int32),
            pltpu.VMEM((1, 32), jnp.int32),
            pltpu.VMEM((1, 32), jnp.int32),
            dma((13,)),
            dma((3, 15)),
            dma((3, 12)),
            dma((16, 2)),
            dma((8, 2)),
            dma((8, 2)),
            dma((2,)),
            dma((2, 2)),
            dma((2, 2)),
            dma((16,)),
            dma((16,)),
            dma,
            dma,
            dma((16,)),
            dma((4,)),
            dma((4,)),
            dma((4,)),
            dma((8,)),
            dma((8,)),
        ],
        compiler_params=pltpu.CompilerParams(
            collective_id=0, has_side_effects=True, vmem_limit_bytes=60 * 1024 * 1024
        ),
        cost_estimate=pl.CostEstimate(flops=10**10, bytes_accessed=8 * 2**20, transcendentals=8 * 10**6),
    )(
        student_hidden, w_keyval, w_query, w_out, norm_gain.reshape(1, -1), student_head.reshape(1, -1), teacher_query,
        teacher_keys, teacher_values, teacher_head.reshape(1, -1), thread_lengths, list_index.reshape(1, -1),
        relevance.reshape(1, -1),
    )
    return out, pooled, tscore[0, :4], div[:, 0]


def solution(mesh):
    return jax.shard_map(
        local,
        mesh=mesh,
        in_specs=(
            P(("dp", "ctx"), None), P("dp", None), P("dp", None), P("dp", None), P(), P(), P("dp", None),
            P(("dp", "ctx"), None), P(("dp", "ctx"), None), P(), P(), P(), P(),
        ),
        out_specs=(P(("dp", "ctx"), None), P("dp", None), P("dp"), P()),
        check_vma=False,
    )
```

time: 1030 us -> 119 us (0.12)
  the two profiles are of different devices: /device:TPU:8 before, /device:TPU:1 now
where the time goes in v1:
time: 119 us
  Pallas kernels  114 us (96%)
  local copies, waits for them, and re-layouts  4.64 us (4%)
    pallas_call x1, Pallas kernels, local(): pl.pallas_call(kernel, out_shape=(jax.ShapeDtypeStruct((ROWS, D), F32), j...  114 us
    unnamed x8, local copies, waits for them, and re-layouts  3.5 us

profile of v1, /device:TPU:1, one launch (start us, length us, event | category | flops | bytes accessed | tf_op | source)
XLA Modules:
  0.0 119.1 jit_solution(12992606220918603461)
XLA Ops:
  0.6 113.8 %shard_map.156 = (f32[256,1024]{1,0:T(8,128)}, f32[4,1024]{1,0:T(4,128)}, f32[1,128]{1,0:T(1,128)}, f32[8,128]{1,0:T(8,128)}) custom-call(bf16[256,1024]{1,0:T(8,128)(2,1)} %hid_in.1, bf16[128,512]{1,0:T(8,128)(2,1)} %wkv_in.1, bf16[128,1024]{1,0:T(8,128)(2,1)} %wq_in.1, bf16[128,1024]{1,0:T(8,128)(2,1)} %wo_in.1, f32[1,1024]{1,0:T(1,128)} %bitcast.8, ...), custom_call_target="tpu_custom_call" | custom-call | flops 10000000000 | bytes 8388608 | tf_op jit(solution)/shard_map/pallas_call | solution.py:554
  114.4 0.0 copy-start.1
  114.4 0.0 copy-start.2
  114.4 0.6 copy-done.2
  115.0 0.5 slice_bitcast_fusion
  115.5 0.0 copy-done.1
  115.5 0.6 slice_reduce_fusion
  116.2 0.0 copy-start
  116.2 2.3 %copy.19 = f32[256,1024]{1,0:T(8,128)} copy(f32[256,1024]{1,0:T(8,128)} %get-tuple-element.16) | data formatting | bytes 2097152
  118.5 0.0 copy-done
  118.5 0.6 copy.20
Async XLA Ops:
  114.4 1.1 copy-start.1
  114.4 0.6 copy-start.2
  116.2 2.3 %copy-start = (f32[4,1024]{1,0:T(4,128)S(1)}, f32[4,1024]{1,0:T(4,128)}, u32[]{:S(2)}) copy-start(f32[4,1024]{1,0:T(4,128)} %get-tuple-element.17) | copy-start | bytes 49156

commit v2 on v1

v2 whole, which is shorter than its diff:
```python
import functools

import jax
import jax.numpy as jnp
from jax import lax
from jax.experimental import pallas as pl
from jax.experimental.pallas import tpu as pltpu
from jax.sharding import PartitionSpec as P

HEADS = 8
KV_HEADS = 2
GROUPS = 4
HD = 128
T_HEADS = 16
ROWS = 256
D = 1024
CHIPS = 8
BIG = -1e30
F32 = jnp.float32
BF16 = jnp.bfloat16
SCALE = HD ** (-0.5)
LOG2E = 1.4426950408889634
MESH = pl.DeviceIdType.MESH


def kernel(
    hid_in, wkv_in, wq_in, wo_in, gain_in, shead_in, tq_in, tk_in, tv_in, thead_in, len_in, list_in, rel_in,
    out_ref, pooled_ref, tscore_ref, div_ref,
    hid, wkv, wq, wo, tk, tv, kvb, relay, qt, att, m_ref, l_ref, acc_ref,
    tbuf, chain, cstage, pbuf, ybuf, sbuf, kv_part,
    gain_ref, shead_ref, tq_ref, thead_ref, len_ref, list_ref, rel_ref,
    lsem, wsend, wrecv, kv_recv, kv_send, sib_send, rev_send, relay_recv, relay_send,
    t_send, t_recv, c_send, c_recv, p_send, p_recv, y_send, y_recv, s_send, s_recv,
):
    dp = lax.axis_index("dp")
    ctx = lax.axis_index("ctx")
    x, zh = dp // 2, dp % 2
    y, pos = ctx // 16, ctx % 16
    c, k = pos // 2, pos % 2
    oz = 1 - zh
    other_dp = 2 * x + oz
    sib_ctx = ctx + 1 - 2 * k
    line = y * 16

    def remote(src, dst, ssem, rsem, to_dp, to_ctx):
        return pltpu.make_async_remote_copy(
            src_ref=src, dst_ref=dst, send_sem=ssem, recv_sem=rsem, device_id=(to_dp, to_ctx), device_id_type=MESH
        )

    def x_peer(d):
        return 2 * ((x + d) % 4) + zh

    def y_peer(d):
        return ((y + d) % 4) * 16 + pos

    thread = dp * 4 + y

    def team(d):
        there = (thread + d) % 32
        return there // 4, (there % 4) * 16 + pos

    lane = 64 * k
    locals_ = [
        pltpu.make_async_copy(hid_in, hid, lsem.at[0]),
        pltpu.make_async_copy(tk_in, tk, lsem.at[1]),
        pltpu.make_async_copy(tv_in, tv, lsem.at[2]),
    ]
    weights = [(wkv_in, wkv), (wq_in, wq), (wo_in, wo)]
    for i, (w_in, w) in enumerate(weights):
        locals_.append(
            pltpu.make_async_copy(w_in.at[pl.ds(lane, 64)], w.at[x, zh, pl.ds(lane, 64)], lsem.at[3 + i])
        )
    small = [
        (gain_in, gain_ref), (shead_in, shead_ref), (tq_in, tq_ref), (thead_in, thead_ref), (len_in, len_ref),
        (list_in, list_ref), (rel_in, rel_ref),
    ]
    small = [pltpu.make_async_copy(src, dst, lsem.at[6 + i]) for i, (src, dst) in enumerate(small)]
    for copy in (locals_[0], locals_[3], locals_[1], locals_[2], locals_[4], locals_[5]):
        copy.start()
    for copy in small:
        copy.start()

    barrier = pltpu.get_barrier_semaphore()

    def greet(to_dp, to_ctx):
        pl.semaphore_signal(barrier, inc=1, device_id=(to_dp, to_ctx), device_id_type=MESH)

    for d in range(1, 16):
        greet(dp, line + (pos + d) % 16)
    for d in range(1, 32):
        greet(*team(d))

    @pl.when(c == 0)
    def _():
        for j in range(4, 8):
            greet(other_dp, line + 2 * j + k)

    @pl.when(c == 7)
    def _():
        for j in range(5):
            greet(other_dp, line + 2 * j + k)

    @pl.when(jnp.logical_and(c >= 1, c <= 4))
    def _():
        greet(other_dp, line + 14 + k)

    @pl.when(jnp.logical_and(c >= 4, c <= 6))
    def _():
        greet(other_dp, line + k)

    @pl.when(c == 1)
    def _():
        greet(other_dp, line + 8 + k)

    @pl.when(c == 4)
    def _():
        greet(other_dp, line + 2 + k)

    def least(value, n):
        return (value + 8 - n) // 8

    more = 3 - 2 * least(c, 1) - least(c, 2) + 2 * least(c, 4) - 2 * least(c, 5) + 4 * least(c, 7)
    pl.semaphore_wait(barrier, 47 + more)

    class Gather:
        def __init__(self, i):
            self.i = i
            self.w_in, self.w = weights[i]
            self.piece = 64 * k + 16 * y

        def sem(self, table, n):
            return table.at[self.i, n]

        def z_copy(self, j):
            w = self.w.at[x, zh, pl.ds(self.piece, 16)]
            return remote(
                self.w_in.at[pl.ds(self.piece, 16)], w, self.sem(wsend, j % 4), self.sem(wrecv, 0),
                other_dp, line + 2 * j + k,
            )

        def z_start(self):
            @pl.when(c == 0)
            def _():
                for j in range(4, 8):
                    self.z_copy(j).start()

            @pl.when(c == 7)
            def _():
                for j in range(4):
                    self.z_copy(j).start()

        def z_recv(self):
            w = self.w.at[x, oz, pl.ds(self.piece, 16)]
            remote(w, w, self.sem(wsend, 0), self.sem(wrecv, 0), other_dp, ctx).wait_recv()

        def own_copy(self, d):
            return remote(
                self.w_in.at[pl.ds(lane, 64)], self.w.at[x, zh, pl.ds(lane, 64)],
                self.sem(wsend, 3 + d), self.sem(wrecv, d), x_peer(d), ctx,
            )

        def own_start(self):
            for d in range(1, 4):
                self.own_copy(d).start()

        def own_recv(self):
            for d in range(1, 4):
                w = self.w.at[(x + 4 - d) % 4, zh, pl.ds(lane, 64)]
                remote(w, w, self.sem(wsend, 0), self.sem(wrecv, d), dp, ctx).wait_recv()

        def other_copy(self, d):
            w = self.w.at[x, oz, pl.ds(self.piece, 16)]
            return remote(w, w, self.sem(wsend, 6 + d), self.sem(wrecv, 3 + d), x_peer(d), ctx)

        def other_start(self):
            for d in range(1, 4):
                self.other_copy(d).start()

        def other_recv(self):
            for d in range(1, 4):
                w = self.w.at[(x + 4 - d) % 4, oz, pl.ds(self.piece, 16)]
                remote(w, w, self.sem(wsend, 0), self.sem(wrecv, 3 + d), dp, ctx).wait_recv()

        def y_copy(self, d):
            w = self.w.at[:, oz, pl.ds(self.piece, 16)]
            return remote(w, w, self.sem(wsend, 9 + d), self.sem(wrecv, 6 + d), dp, y_peer(d))

        def y_start(self):
            for d in range(1, 4):
                self.y_copy(d).start()

        def y_recv(self):
            for d in range(1, 4):
                w = self.w.at[:, oz, pl.ds(64 * k + 16 * ((y + 4 - d) % 4), 16)]
                remote(w, w, self.sem(wsend, 0), self.sem(wrecv, 6 + d), dp, ctx).wait_recv()

        def sib_copy(self, half, n):
            w = self.w.at[:, half, pl.ds(lane, 64)]
            return remote(w, w, self.sem(wsend, 13 + n), self.sem(wrecv, 10 + n), dp, sib_ctx)

        def sib_recv(self, half, n):
            w = self.w.at[:, half, pl.ds(64 - lane, 64)]
            remote(w, w, self.sem(wsend, 0), self.sem(wrecv, 10 + n), dp, ctx).wait_recv()

        def finish(self):
            @pl.when(c == 0)
            def _():
                for j in range(4, 8):
                    self.z_copy(j).wait_send()

            @pl.when(c == 7)
            def _():
                for j in range(4):
                    self.z_copy(j).wait_send()

            for d in range(1, 4):
                self.own_copy(d).wait_send()
                self.other_copy(d).wait_send()
                self.y_copy(d).wait_send()
            self.sib_copy(zh, 0).wait_send()
            self.sib_copy(oz, 1).wait_send()

    gkv, gq, go = Gather(0), Gather(1), Gather(2)
    gkv.z_start()
    gkv.own_start()

    for copy in small:
        copy.wait()
    length = len_ref[thread]
    slot_row = lax.broadcasted_iota(jnp.int32, (4, 2048), 0) == y
    own_q = jnp.sum(jnp.where(slot_row, tq_ref[...].astype(F32), 0.0), axis=0, keepdims=True)
    head_of = lax.broadcasted_iota(jnp.int32, (T_HEADS, 2048), 1) // HD
    diagonal = head_of == lax.broadcasted_iota(jnp.int32, (T_HEADS, 2048), 0)
    q_heads = jnp.where(diagonal, own_q, 0.0).astype(BF16)
    locals_[1].wait()
    ts = lax.dot_general(q_heads, tk[...], (((1,), (1,)), ((), ())), preferred_element_type=F32) * SCALE
    t_valid = pos * ROWS + lax.broadcasted_iota(jnp.int32, (T_HEADS, ROWS), 1) < length
    ts = jnp.where(t_valid, ts, BIG)
    t_best = jnp.max(ts, axis=1, keepdims=True)
    t_weights = jnp.where(t_valid, jnp.exp(ts - t_best), 0.0)
    t_total = jnp.sum(t_weights, axis=1, keepdims=True)
    locals_[2].wait()
    t_out = jnp.dot(t_weights.astype(BF16), tv[...], preferred_element_type=F32)
    t_sum = jnp.sum(jnp.where(diagonal, t_out * thead_ref[...], 0.0), axis=1, keepdims=True)
    eye = lax.broadcasted_iota(jnp.int32, (T_HEADS, 128), 0) == lax.broadcasted_iota(jnp.int32, (T_HEADS, 128), 1)

    def row_of(column):
        return jnp.sum(jnp.where(eye, column, 0.0), axis=0, keepdims=True)

    tbuf[pos] = jnp.concatenate([row_of(t_best), row_of(t_total), row_of(t_sum)], axis=1)

    def t_copy(d):
        return remote(tbuf.at[pos], tbuf.at[pos], t_send.at[d], t_recv.at[d], dp, line + (pos + d) % 16)

    gkv.z_recv()
    gkv.other_start()
    gq.z_start()
    gkv.own_recv()
    locals_[3].wait()
    gkv.sib_copy(zh, 0).start()
    gq.own_start()
    gkv.other_recv()
    gkv.y_start()
    for d in range(1, 16):
        t_copy(d).start()
    locals_[0].wait()

    def hid_half(half):
        parts = [hid[:, pl.ds(pl.multiple_of((2 * i + half) * 128, 128), 128)] for i in range(4)]
        return jnp.concatenate(parts, axis=1)

    gkv.sib_recv(zh, 0)
    kv_part[...] = jnp.dot(hid_half(zh), wkv[:, zh].reshape(512, 512), preferred_element_type=F32)
    gkv.y_recv()
    gkv.sib_copy(oz, 1).start()
    gq.z_recv()
    gq.other_start()
    gkv.sib_recv(oz, 1)
    keyval = kv_part[...] + jnp.dot(hid_half(oz), wkv[:, oz].reshape(512, 512), preferred_element_type=F32)
    keyval = keyval.astype(BF16)
    own = 2 * c + k

    def hand(b, q, ssem, to_ctx):
        ref = kvb.at[2 * b + k, q]
        return remote(ref, ref, ssem.at[b, q], kv_recv.at[2 * b + k, q], dp, to_ctx)

    def ring_copy(b, q):
        return hand(b, q, kv_send, ctx + 2)

    def back_copy(b, q):
        return hand(b, q, kv_send, ctx - 2)

    def sib_copy(b, q):
        return hand(b, q, sib_send, sib_ctx)

    def kv_wait(block, q):
        ref = kvb.at[block, q]
        remote(ref, ref, kv_send.at[0, 0], kv_recv.at[block, q], dp, ctx).wait_recv()

    def rev_copy(q):
        return remote(
            kvb.at[own, q], relay.at[c, q], rev_send.at[q], relay_recv.at[c, q], other_dp, line + 8 + k
        )

    def relay_copy(r, q):
        return remote(
            relay.at[r, q], kvb.at[2 * r + k, q], relay_send.at[r, q], kv_recv.at[2 * r + k, q], other_dp, line + 14 + k
        )

    def passes_on(b):
        gap = jnp.logical_or(jnp.logical_and(b == 0, c >= 5), jnp.logical_and(b == 1, c >= 6))
        return jnp.logical_and(c < 7, jnp.logical_not(gap))

    for h in range(KV_HEADS):
        kvb[own, 2 * h] = keyval[:, h * HD : (h + 1) * HD]
        for part in range(2):
            value = keyval[part * 128 : (part + 1) * 128, (KV_HEADS + h) * HD : (KV_HEADS + h + 1) * HD]
            kvb[own, 2 * h + 1, pl.ds(part * 128, 128)] = value.T
        for q in (2 * h, 2 * h + 1):

            @pl.when(c < 7)
            def _():
                ring_copy(c, q).start()

            @pl.when(c == 0)
            def _():
                rev_copy(q).start()

            sib_copy(c, q).start()

    def block_at(s):
        last = -4 * least(s, 3) + 5 * least(s, 4) - least(s, 6) + 2 * least(s, 7)
        before = -least(s, 5) + 2 * least(s, 6)
        return c - s + last * least(c, 7) + before * (least(c, 6) - least(c, 7))

    def forward(s, h):
        b = block_at(s)

        @pl.when(s <= c)
        def _():
            for q in (2 * h, 2 * h + 1):
                kv_wait(2 * b + k, q)

                @pl.when(passes_on(b))
                def _():
                    ring_copy(b, q).start()

                @pl.when(jnp.logical_and(c == 7, b == 0))
                def _():
                    back_copy(b, q).start()

                sib_copy(b, q).start()

    def relay_on(r, h):
        @pl.when(c == 4)
        def _():
            for q in (2 * h, 2 * h + 1):
                ref = relay.at[r, q]
                remote(ref, ref, rev_send.at[q], relay_recv.at[r, q], dp, ctx).wait_recv()
                relay_copy(r, q).start()

    def attend(b, h, diag):
        kp = jnp.concatenate([kvb[2 * b, 2 * h], kvb[2 * b + 1, 2 * h]], axis=0)
        v0, v1 = kvb[2 * b, 2 * h + 1], kvb[2 * b + 1, 2 * h + 1]
        vt = jnp.concatenate([v0[:128], v0[128:], v1[:128], v1[128:]], axis=1)

        def score(g):
            return jnp.dot(kp, qt[h, g], preferred_element_type=F32)

        ahead = score(0)
        for g in range(GROUPS):
            i = h * GROUPS + g
            s = ahead * (SCALE * LOG2E)
            if g + 1 < GROUPS:
                ahead = score(g + 1)
            if diag:
                key = lax.broadcasted_iota(jnp.int32, (2 * ROWS, ROWS), 0)
                row = lax.broadcasted_iota(jnp.int32, (2 * ROWS, ROWS), 1)
                s = jnp.where(key <= k * ROWS + row, s, BIG)
            best = jnp.max(s, axis=0, keepdims=True)
            if not diag:
                old = m_ref[i]
                best = jnp.maximum(old, best)
                carry = jnp.exp2(old - best)
            p = jnp.exp2(s - best)
            total = jnp.sum(p, axis=0, keepdims=True)
            out = jnp.dot(vt, p.astype(BF16), preferred_element_type=F32)
            m_ref[i] = best
            if diag:
                l_ref[i] = total
                acc_ref[i] = out
            else:
                l_ref[i] = l_ref[i] * carry + total
                acc_ref[i] = acc_ref[i] * carry + out

    gq.other_recv()
    gq.y_start()
    gq.own_recv()
    locals_[4].wait()
    gq.sib_copy(zh, 0).start()
    go.z_start()
    go.own_start()
    for h in range(KV_HEADS):
        forward(1, h)
        relay_on(0, h)

    @pl.when(c == 1)
    def _():
        for q in range(4):
            rev_copy(q).start()

    gq.y_recv()
    gq.sib_copy(oz, 1).start()
    forward(2, 0)
    go.z_recv()
    go.other_start()
    gq.sib_recv(zh, 0)
    gq.sib_recv(oz, 1)
    query = jnp.dot(hid[...], wq[...].reshape(D, HEADS * HD), preferred_element_type=F32).astype(BF16)
    for i in range(HEADS):
        qt[i // GROUPS, i % GROUPS] = query[:, i * HD : (i + 1) * HD].T
    forward(2, 1)
    for h in range(KV_HEADS):
        for q in (2 * h, 2 * h + 1):
            kv_wait(2 * c + 1 - k, q)
        attend(c, h, True)
    go.own_recv()
    locals_[5].wait()
    go.sib_copy(zh, 0).start()
    go.other_recv()
    go.y_start()

    def first_part(u):
        return u - 1 - (9 - u) * (1 - (u + 7) // 16)

    def part(a, carry):
        pair, h = a // 2, a % 2

        @pl.when(pair <= c)
        def _():
            b = block_at(pair)
            for j in range(2):
                kv_wait(2 * b + 1 - k, 2 * h + j)
            attend(b, h, False)

        return carry

    def step(s, carry):
        for h in range(KV_HEADS):
            forward(s, h)

            @pl.when(s == 3)
            def _():
                relay_on(1, h)

            u = 2 * s + h
            lax.fori_loop(first_part(u), first_part(u + 1), part, 0)

        @pl.when(s == 5)
        def _():
            go.y_recv()
            go.sib_copy(oz, 1).start()

        return carry

    lax.fori_loop(3, 8, step, 0)
    part(15, 0)

    for i in range(HEADS):
        att[:, i * HD : (i + 1) * HD] = (acc_ref[i] / l_ref[i]).astype(BF16).T
    go.sib_recv(zh, 0)
    go.sib_recv(oz, 1)
    hidden = hid[...].astype(F32) + jnp.dot(att[...], wo[...].reshape(D, D), preferred_element_type=F32)
    valid = pos * ROWS + lax.broadcasted_iota(jnp.int32, (ROWS, 1), 0) < length
    rate = jnp.where(valid, lax.rsqrt(jnp.mean(hidden * hidden, axis=1, keepdims=True) + 1e-05), 0.0)
    part = jnp.sum(hidden * rate, axis=0, keepdims=True) * gain_ref[...]
    out_ref[...] = jnp.where(valid, hidden, 0.0)

    def chain_copy():
        return remote(cstage, chain, c_send, c_recv, dp, ctx + 2)

    @pl.when(c == 0)
    def _():
        chain[...] = jnp.zeros_like(chain)

    @pl.when(jnp.logical_and(c >= 1, c <= 5))
    def _():
        remote(chain, chain, c_send, c_recv, dp, ctx).wait_recv()

    @pl.when(c <= 4)
    def _():
        cstage[...] = part + chain[...]
        chain_copy().start()

    def p_copy(r, d):
        return remote(pbuf.at[r], pbuf.at[r], p_send.at[d], p_recv.at[r], dp, line + (pos + d) % 16)

    root = 2 * (c - 5) + k

    @pl.when(c == 5)
    def _():
        pbuf[root] = part + chain[...]

    @pl.when(c >= 6)
    def _():
        pbuf[root] = part

    @pl.when(c >= 5)
    def _():
        for d in range(1, 16):
            p_copy(root, d).start()

    for d in range(1, 16):
        ref = tbuf.at[(pos + 16 - d) % 16]
        remote(ref, ref, t_send.at[0], t_recv.at[d], dp, ctx).wait_recv()
    stats = jnp.concatenate([tbuf[i] for i in range(16)], axis=0)
    bests = stats[:, :128]
    factor = jnp.exp(bests - jnp.max(bests, axis=0, keepdims=True))
    total = jnp.sum(stats[:, 128:256] * factor, axis=0, keepdims=True)
    above = jnp.sum(stats[:, 256:] * factor, axis=0, keepdims=True)
    in_heads = lax.broadcasted_iota(jnp.int32, (1, 128), 1) < T_HEADS
    t_score = jnp.sum(jnp.where(in_heads, above / jnp.where(in_heads, total, 1.0), 0.0), axis=1, keepdims=True)

    for r in range(6):

        @pl.when(pos != 10 + r)
        def _():
            ref = pbuf.at[r]
            remote(ref, ref, c_send, p_recv.at[r], dp, ctx).wait_recv()

    pooled_sum = ((pbuf[0] + pbuf[1]) + (pbuf[2] + pbuf[3])) + (pbuf[4] + pbuf[5])
    pooled = pooled_sum / length.astype(F32)
    ybuf[y] = pooled
    student = jnp.sum(pooled * shead_ref[...], axis=1, keepdims=True)
    lanes = lax.broadcasted_iota(jnp.int32, (1, 128), 1)
    sbuf[thread] = jnp.where(lanes == thread, student, 0.0) + jnp.where(lanes == 64 + thread, t_score, 0.0)

    def s_copy(d):
        return remote(sbuf.at[thread], sbuf.at[thread], s_send.at[d], s_recv.at[d], *team(d))

    def y_copy(d):
        return remote(ybuf.at[y], ybuf.at[y], y_send.at[d], y_recv.at[d], dp, y_peer(d))

    for d in range(1, 32):
        s_copy(d).start()
    for d in range(1, 4):
        y_copy(d).start()

    def sent(b, carry):
        for q in range(4):

            @pl.when(jnp.logical_or(passes_on(b), jnp.logical_and(c == 7, b == 0)))
            def _():
                ring_copy(b, q).wait_send()

            sib_copy(b, q).wait_send()
        return carry

    lax.fori_loop(0, c + 1, sent, 0)

    @pl.when(c <= 1)
    def _():
        for q in range(4):
            rev_copy(q).wait_send()

    @pl.when(c == 4)
    def _():
        for r in range(2):
            for q in range(4):
                relay_copy(r, q).wait_send()

    for gather in (gkv, gq, go):
        gather.finish()
    for d in range(1, 16):
        t_copy(d).wait_send()

    @pl.when(c <= 4)
    def _():
        chain_copy().wait_send()

    @pl.when(c >= 5)
    def _():
        for d in range(1, 16):
            p_copy(root, d).wait_send()

    for d in range(1, 4):
        y_copy(d).wait_send()

    for d in range(1, 4):
        ref = ybuf.at[(y + 4 - d) % 4]
        remote(ref, ref, y_send.at[0], y_recv.at[d], dp, ctx).wait_recv()
    for i in range(4):
        pooled_ref[i : i + 1, :] = ybuf[i]
    for d in range(1, 32):
        ref = sbuf.at[(thread + 32 - d) % 32]
        remote(ref, ref, s_send.at[0], s_recv.at[d], dp, ctx).wait_recv()
    every = jnp.sum(sbuf[...].reshape(32, 128), axis=0, keepdims=True)
    member_t = lax.broadcasted_iota(jnp.int32, (4, 128), 1) == 64 + dp * 4 + lax.broadcasted_iota(jnp.int32, (4, 128), 0)
    t_column = jnp.sum(jnp.where(member_t, every, 0.0), axis=1, keepdims=True)
    eye4 = lax.broadcasted_iota(jnp.int32, (4, 4), 0) == lax.broadcasted_iota(jnp.int32, (4, 4), 1)
    tscore_ref[...] = jnp.sum(jnp.where(eye4, t_column, 0.0), axis=0, keepdims=True)

    threads = list_ref.shape[1]
    student_all, teacher_all = every[:, :threads], every[:, 64 : 64 + threads]
    target = teacher_all + rel_ref[...].astype(F32)
    member = lax.broadcasted_iota(jnp.int32, (8, threads), 0) == list_ref[...]

    def log_soft(logits):
        masked = jnp.where(member, logits, BIG)
        top = jnp.max(masked, axis=1, keepdims=True)
        shifted = jnp.where(member, jnp.exp(masked - top), 0.0)
        return masked - top - jnp.log(jnp.sum(shifted, axis=1, keepdims=True))

    target_log = log_soft(target)
    student_log = log_soft(student_all)
    target_prob = jnp.where(member, jnp.exp(target_log), 0.0)
    terms = jnp.where(member, target_prob * (target_log - student_log), 0.0)
    div_column = jnp.sum(terms, axis=1, keepdims=True)
    eye8 = lax.broadcasted_iota(jnp.int32, (8, 8), 0) == lax.broadcasted_iota(jnp.int32, (8, 8), 1)
    div_ref[...] = jnp.sum(jnp.where(eye8, div_column, 0.0), axis=0, keepdims=True)

    for d in range(1, 32):
        s_copy(d).wait_send()


def place(out, pooled, tscore, div, out_ref, pooled_ref, tscore_ref, div_ref):
    out_ref[...] = out[...]
    pooled_ref[...] = pooled[...]
    tscore_ref[...] = tscore[...]
    div_ref[...] = div[...]


def local(
    student_hidden, w_query, w_keyval, w_out, norm_gain, student_head, teacher_query, teacher_keys, teacher_values,
    teacher_head, thread_lengths, list_index, relevance,
):
    vmem = pl.BlockSpec(memory_space=pltpu.VMEM)
    anywhere = pl.BlockSpec(memory_space=pl.ANY)
    dma = pltpu.SemaphoreType.DMA
    out, pooled, tscore, div = pl.pallas_call(
        kernel,
        out_shape=(
            jax.ShapeDtypeStruct((ROWS, D), F32),
            jax.ShapeDtypeStruct((4, D), F32),
            jax.ShapeDtypeStruct((1, 4), F32),
            jax.ShapeDtypeStruct((1, 8), F32),
        ),
        in_specs=[anywhere] * 13,
        out_specs=(vmem,) * 4,
        scratch_shapes=[
            pltpu.VMEM((ROWS, D), BF16),
            pltpu.VMEM((4, 2, 128, 512), BF16),
            pltpu.VMEM((4, 2, 128, D), BF16),
            pltpu.VMEM((4, 2, 128, D), BF16),
            pltpu.VMEM((ROWS, 2048), BF16),
            pltpu.VMEM((ROWS, 2048), BF16),
            pltpu.VMEM((16, 4, 256, 128), BF16),
            pltpu.VMEM((2, 4, 256, 128), BF16),
            pltpu.VMEM((KV_HEADS, GROUPS, HD, ROWS), BF16),
            pltpu.VMEM((ROWS, D), BF16),
            pltpu.VMEM((HEADS, 1, ROWS), F32),
            pltpu.VMEM((HEADS, 1, ROWS), F32),
            pltpu.VMEM((HEADS, HD, ROWS), F32),
            pltpu.VMEM((16, 1, 384), F32),
            pltpu.VMEM((1, D), F32),
            pltpu.VMEM((1, D), F32),
            pltpu.VMEM((6, 1, D), F32),
            pltpu.VMEM((4, 1, D), F32),
            pltpu.VMEM((32, 1, 128), F32),
            pltpu.VMEM((ROWS, 512), F32),
            pltpu.VMEM((1, D), F32),
            pltpu.VMEM((1, D), F32),
            pltpu.VMEM((4, 2048), BF16),
            pltpu.VMEM((1, 2048), F32),
            pltpu.SMEM((32,), jnp.int32),
            pltpu.VMEM((1, 32), jnp.int32),
            pltpu.VMEM((1, 32), jnp.int32),
            dma((13,)),
            dma((3, 15)),
            dma((3, 12)),
            dma((16, 4)),
            dma((8, 4)),
            dma((8, 4)),
            dma((4,)),
            dma((2, 4)),
            dma((2, 4)),
            dma((16,)),
            dma((16,)),
            dma,
            dma,
            dma((16,)),
            dma((6,)),
            dma((4,)),
            dma((4,)),
            dma((32,)),
            dma((32,)),
        ],
        compiler_params=pltpu.CompilerParams(
            collective_id=0, has_side_effects=True, vmem_limit_bytes=60 * 1024 * 1024
        ),
        cost_estimate=pl.CostEstimate(flops=10**10, bytes_accessed=8 * 2**20, transcendentals=8 * 10**6),
    )(
        student_hidden, w_keyval, w_query, w_out, norm_gain.reshape(1, -1), student_head.reshape(1, -1), teacher_query,
        teacher_keys, teacher_values, teacher_head.reshape(1, -1), thread_lengths, list_index.reshape(1, -1),
        relevance.reshape(1, -1),
    )
    out, pooled, tscore, div = pl.pallas_call(
        place,
        out_shape=tuple(jax.ShapeDtypeStruct(a.shape, a.dtype) for a in (out, pooled, tscore, div)),
        in_specs=[vmem] * 4,
        out_specs=(vmem,) * 4,
        compiler_params=pltpu.CompilerParams(vmem_limit_bytes=60 * 1024 * 1024),
    )(out, pooled, tscore, div)
    return out, pooled, tscore.reshape(4), div.reshape(8)


def solution(mesh):
    return jax.shard_map(
        local,
        mesh=mesh,
        in_specs=(
            P(("dp", "ctx"), None), P("dp", None), P("dp", None), P("dp", None), P(), P(), P("dp", None),
            P(("dp", "ctx"), None), P(("dp", "ctx"), None), P(), P(), P(), P(),
        ),
        out_specs=(P(("dp", "ctx"), None), P("dp", None), P("dp"), P()),
        check_vma=False,
    )
```

time: 119 us -> 99.9 us (0.84)
  Pallas kernels: 114 us -> 99.1 us
  local copies, waits for them, and re-layouts: 4.64 us -> 0 us
    pallas_call x1, Pallas kernels: 114 us -> 96.8 us  [local(): pl.pallas_call(kernel, out_shape=(jax.ShapeDtypeStruct((ROWS, D), F32), j...]
    unnamed x8 -> x0, local copies, waits for them, and re-layouts: 3.5 us -> none
    pallas_call x0 -> x1, Pallas kernels: none -> 2.29 us  [local(): pl.pallas_call(place, out_shape=tuple((jax.ShapeDtypeStruct(a.shape, a.dt...]
where the time goes in v2:
time: 99.9 us; the launch traced here: 99.7 us
  Pallas kernels  99.1 us (99%)
    pallas_call x1, Pallas kernels, local(): pl.pallas_call(kernel, out_shape=(jax.ShapeDtypeStruct((ROWS, D), F32), j...  96.8 us
    pallas_call x1, Pallas kernels, local(): pl.pallas_call(place, out_shape=tuple((jax.ShapeDtypeStruct(a.shape, a.dt...  2.29 us

profile of v2, /device:TPU:1, one launch (start us, length us, event | category | flops | bytes accessed | tf_op | source)
XLA Modules:
  0.0 99.7 jit_solution(7902612018267892872)
XLA Ops:
  0.6 96.8 %shard_map.156 = (f32[256,1024]{1,0:T(8,128)}, f32[4,1024]{1,0:T(4,128)}, f32[1,4]{1,0:T(1,128)}, f32[1,8]{1,0:T(1,128)}) custom-call(bf16[256,1024]{1,0:T(8,128)(2,1)} %hid_in.1, bf16[128,512]{1,0:T(8,128)(2,1)} %wkv_in.1, bf16[128,1024]{1,0:T(8,128)(2,1)} %wq_in.1, bf16[128,1024]{1,0:T(8,128)(2,1)} %wo_in.1, f32[1,1024]{1,0:T(1,128)} %bitcast.8, ...), custom_call_target="tpu_custom_call" | custom-call | flops 10000000000 | bytes 8388608 | tf_op jit(solution)/shard_map/pallas_call | solution.py:640
  97.5 2.3 %shard_map.157 = (f32[256,1024]{1,0:T(8,128)}, f32[4,1024]{1,0:T(4,128)}, f32[1,4]{1,0:T(1,128)}, f32[1,8]{1,0:T(1,128)}) custom-call(f32[256,1024]{1,0:T(8,128)} %get-tuple-element.12.out, f32[4,1024]{1,0:T(4,128)} %get-tuple-element.13.pooled, f32[1,4]{1,0:T(1,128)} %get-tuple-element.14.tscore, f32[1,8]{1,0:T(1,128)} %get-tuple-element.15.div), custom_call_target="tpu_custom_call" | custom-call | tf_op jit(solution)/shard_map/pallas_call | solution.py:707

commit v3 on v2

v3 whole, which is shorter than its diff:
```python
import functools

import jax
import jax.numpy as jnp
from jax import lax
from jax.experimental import pallas as pl
from jax.experimental.pallas import tpu as pltpu
from jax.sharding import PartitionSpec as P

HEADS = 8
KV_HEADS = 2
GROUPS = 4
HD = 128
T_HEADS = 16
ROWS = 256
D = 1024
CHIPS = 8
BIG = -1e30
F32 = jnp.float32
BF16 = jnp.bfloat16
SCALE = HD ** (-0.5)
LOG2E = 1.4426950408889634
MESH = pl.DeviceIdType.MESH


def kernel(
    hid_in, wkv_in, wq_in, wo_in, gain_in, shead_in, tq_in, tk_in, tv_in, thead_in, len_in, list_in, rel_in,
    out_ref, pooled_ref, tscore_ref, div_ref,
    hid, wk, wv, wq, wo, tk, tv, kvb, relay, qt, att, m_ref, l_ref, acc_ref,
    tsib, tbuf, trow, cbuf, cstage, pbuf, rbuf, ybuf, sbuf, kv_part,
    gain_ref, shead_ref, tq_ref, thead_ref, len_ref, list_ref, rel_ref,
    lsem, wsend, wrecv, kv_recv, kv_send, sib_send, rev_send, relay_recv, relay_send,
    t_send, t_recv, c_send, c_recv, p_send, p_recv, r_send, r_recv, y_send, y_recv, s_send, s_recv,
):
    dp = lax.axis_index("dp")
    ctx = lax.axis_index("ctx")
    x, zh = dp // 2, dp % 2
    y, pos = ctx // 16, ctx % 16
    c, k = pos // 2, pos % 2
    oz = 1 - zh
    other_dp = 2 * x + oz
    sib_ctx = ctx + 1 - 2 * k
    line = y * 16

    def remote(src, dst, ssem, rsem, to_dp, to_ctx):
        return pltpu.make_async_remote_copy(
            src_ref=src, dst_ref=dst, send_sem=ssem, recv_sem=rsem, device_id=(to_dp, to_ctx), device_id_type=MESH
        )

    def x_peer(d):
        return 2 * ((x + d) % 4) + zh

    def y_peer(d):
        return ((y + d) % 4) * 16 + pos

    thread = dp * 4 + y

    lane = 64 * k
    locals_ = [
        pltpu.make_async_copy(hid_in, hid, lsem.at[0]),
        pltpu.make_async_copy(tk_in, tk, lsem.at[1]),
        pltpu.make_async_copy(tv_in, tv, lsem.at[2]),
    ]
    weights = [(wkv_in.at[:, pl.ds(0, 256)], wk), (wkv_in.at[:, pl.ds(256, 256)], wv), (wq_in, wq), (wo_in, wo)]
    for i, (w_in, w) in enumerate(weights):
        locals_.append(
            pltpu.make_async_copy(w_in.at[pl.ds(lane, 64)], w.at[x, zh, pl.ds(lane, 64)], lsem.at[3 + i])
        )
    small = [
        (gain_in, gain_ref), (shead_in, shead_ref), (tq_in, tq_ref), (thead_in, thead_ref), (len_in, len_ref),
        (list_in, list_ref), (rel_in, rel_ref),
    ]
    small = [pltpu.make_async_copy(src, dst, lsem.at[7 + i]) for i, (src, dst) in enumerate(small)]
    for copy in [locals_[0]] + locals_[3:] + locals_[1:3]:
        copy.start()
    for copy in small:
        copy.start()

    barrier = pltpu.get_barrier_semaphore()

    def greet(to_dp, to_ctx):
        pl.semaphore_signal(barrier, inc=1, device_id=(to_dp, to_ctx), device_id_type=MESH)

    greet(dp, sib_ctx)
    for d in range(1, 4):
        greet(dp, y_peer(d))
        greet(x_peer(d), ctx)

    @pl.when(c < 7)
    def _():
        greet(dp, ctx + 2)

    @pl.when(c > 0)
    def _():
        greet(dp, ctx - 2)

    @pl.when(c == 0)
    def _():
        for j in range(4, 8):
            greet(other_dp, line + 2 * j + k)

    @pl.when(c == 7)
    def _():
        for j in range(5):
            greet(other_dp, line + 2 * j + k)

    @pl.when(jnp.logical_and(c >= 1, c <= 4))
    def _():
        greet(other_dp, line + 14 + k)

    @pl.when(jnp.logical_and(c >= 4, c <= 6))
    def _():
        greet(other_dp, line + k)

    @pl.when(c == 1)
    def _():
        greet(other_dp, line + 8 + k)

    @pl.when(c == 4)
    def _():
        greet(other_dp, line + 2 + k)

    def least(value, n):
        return (value + 8 - n) // 8

    @pl.when(c == 6)
    def _():
        for j in range(5):
            greet(dp, line + 2 * j + k)

    more = 3 - 2 * least(c, 1) - least(c, 2) + 2 * least(c, 4) - 2 * least(c, 5) + 4 * least(c, 7)
    pl.semaphore_wait(barrier, 10 + least(c, 1) - least(c, 5) - least(c, 7) + more)

    class Gather:
        def __init__(self, i):
            self.i = i
            self.w_in, self.w = weights[i]
            self.piece = 64 * k + 16 * y
            self.ring = i >= 2

        def sem(self, table, n):
            return table.at[self.i, n]

        def z_copy(self, j):
            w = self.w.at[x, zh, pl.ds(self.piece, 16)]
            return remote(
                self.w_in.at[pl.ds(self.piece, 16)], w, self.sem(wsend, j % 4), self.sem(wrecv, 0),
                other_dp, line + 2 * j + k,
            )

        def z_start(self):
            @pl.when(c == 0)
            def _():
                for j in range(4, 8):
                    self.z_copy(j).start()

            @pl.when(c == 7)
            def _():
                for j in range(4):
                    self.z_copy(j).start()

        def z_recv(self):
            w = self.w.at[x, oz, pl.ds(self.piece, 16)]
            remote(w, w, self.sem(wsend, 0), self.sem(wrecv, 0), other_dp, ctx).wait_recv()

        def own_part(self, at, first=0, rows=64):
            return self.w.at[(x + at) % 4, zh, pl.ds(lane + first, rows)]

        def own_copies(self):
            src = self.w_in.at[pl.ds(lane, 64)]
            hops = (1, 3) if self.ring else (1, 2, 3)
            return [
                remote(src, self.own_part(0), self.sem(wsend, 3 + d), self.sem(wrecv, d), x_peer(d), ctx) for d in hops
            ]

        def own_relays(self):
            left, right = self.own_part(3, 0, 32), self.own_part(1, 32, 32)
            return [
                remote(left, left, self.sem(wsend, 5), self.sem(wrecv, 2), x_peer(1), ctx),
                remote(right, right, self.sem(wsend, 15), self.sem(wrecv, 12), x_peer(3), ctx),
            ]

        def own_start(self):
            for copy in self.own_copies():
                copy.start()

        def arrived(self, w, n):
            remote(w, w, self.sem(wsend, 0), self.sem(wrecv, n), dp, ctx).wait_recv()

        def own_mid(self):
            relays = self.own_relays()
            self.arrived(self.own_part(3), 1)
            relays[0].start()
            self.arrived(self.own_part(1), 3)
            relays[1].start()

        def own_recv(self):
            if self.ring:
                self.arrived(self.own_part(2, 0, 32), 2)
                self.arrived(self.own_part(2, 32, 32), 12)
            else:
                for d in range(1, 4):
                    self.arrived(self.own_part(4 - d), d)

        def other_copy(self, d):
            w = self.w.at[x, oz, pl.ds(self.piece, 16)]
            return remote(w, w, self.sem(wsend, 6 + d), self.sem(wrecv, 3 + d), x_peer(d), ctx)

        def other_start(self):
            for d in range(1, 4):
                self.other_copy(d).start()

        def other_recv(self):
            for d in range(1, 4):
                w = self.w.at[(x + 4 - d) % 4, oz, pl.ds(self.piece, 16)]
                remote(w, w, self.sem(wsend, 0), self.sem(wrecv, 3 + d), dp, ctx).wait_recv()

        def y_part(self, at, first=0, count=4):
            return self.w.at[pl.ds(first, count), oz, pl.ds(64 * k + 16 * ((y + at) % 4), 16)]

        def y_copies(self):
            src = self.y_part(0)
            hops = (1, 3) if self.ring else (1, 2, 3)
            return [remote(src, src, self.sem(wsend, 9 + d), self.sem(wrecv, 6 + d), dp, y_peer(d)) for d in hops]

        def y_relays(self):
            left, right = self.y_part(3, 0, 2), self.y_part(1, 2, 2)
            return [
                remote(left, left, self.sem(wsend, 11), self.sem(wrecv, 8), dp, y_peer(1)),
                remote(right, right, self.sem(wsend, 16), self.sem(wrecv, 13), dp, y_peer(3)),
            ]

        def y_start(self):
            for copy in self.y_copies():
                copy.start()

        def y_mid(self):
            relays = self.y_relays()
            self.arrived(self.y_part(3), 7)
            relays[0].start()
            self.arrived(self.y_part(1), 9)
            relays[1].start()

        def y_recv(self):
            if self.ring:
                self.arrived(self.y_part(2, 0, 2), 8)
                self.arrived(self.y_part(2, 2, 2), 13)
            else:
                for d in range(1, 4):
                    self.arrived(self.y_part(4 - d), 6 + d)

        def sib_copy(self, half, n):
            w = self.w.at[:, half, pl.ds(lane, 64)]
            return remote(w, w, self.sem(wsend, 13 + n), self.sem(wrecv, 10 + n), dp, sib_ctx)

        def sib_recv(self, half, n):
            w = self.w.at[:, half, pl.ds(64 - lane, 64)]
            remote(w, w, self.sem(wsend, 0), self.sem(wrecv, 10 + n), dp, ctx).wait_recv()

        def finish(self):
            @pl.when(c == 0)
            def _():
                for j in range(4, 8):
                    self.z_copy(j).wait_send()

            @pl.when(c == 7)
            def _():
                for j in range(4):
                    self.z_copy(j).wait_send()

            copies = self.own_copies() + self.y_copies() + [self.other_copy(d) for d in range(1, 4)]
            for copy in copies + (self.own_relays() + self.y_relays() if self.ring else []):
                copy.wait_send()
            self.sib_copy(zh, 0).wait_send()
            self.sib_copy(oz, 1).wait_send()

    for copy in small:
        copy.wait()
    length = len_ref[thread]
    gk, gv, gq, go = (Gather(i) for i in range(4))

    for gather in (gk, gv):
        gather.z_start()
        gather.own_start()
    for gather in (gk, gv):
        gather.z_recv()
        gather.other_start()
    gq.z_start()
    for gather, copy in ((gk, locals_[3]), (gv, locals_[4])):
        gather.own_recv()
        copy.wait()
        gather.sib_copy(zh, 0).start()
    for gather in (gk, gv):
        gather.other_recv()
        gather.y_start()
    gq.own_start()
    locals_[0].wait()

    def project(half, w):
        parts = [hid[:, pl.ds(pl.multiple_of((2 * i + half) * 128, 128), 128)] for i in range(4)]
        return jnp.dot(jnp.concatenate(parts, axis=1), w[:, half].reshape(512, 256), preferred_element_type=F32)

    gk.sib_recv(zh, 0)
    kv_part[0] = project(zh, wk)
    gv.sib_recv(zh, 0)
    kv_part[1] = project(zh, wv)
    for gather in (gk, gv):
        gather.y_recv()
        gather.sib_copy(oz, 1).start()
    gq.z_recv()
    gq.other_start()
    own = 2 * c + k

    def hand(b, q, ssem, to_ctx):
        ref = kvb.at[2 * b + k, q]
        return remote(ref, ref, ssem.at[b, q], kv_recv.at[2 * b + k, q], dp, to_ctx)

    def ring_copy(b, q):
        return hand(b, q, kv_send, ctx + 2)

    def back_copy(b, q):
        return hand(b, q, kv_send, ctx - 2)

    def sib_copy(b, q):
        return hand(b, q, sib_send, sib_ctx)

    def kv_wait(block, q):
        ref = kvb.at[block, q]
        remote(ref, ref, kv_send.at[0, 0], kv_recv.at[block, q], dp, ctx).wait_recv()

    def rev_copy(q):
        return remote(
            kvb.at[own, q], relay.at[c, q], rev_send.at[q], relay_recv.at[c, q], other_dp, line + 8 + k
        )

    def relay_copy(r, q):
        return remote(
            relay.at[r, q], kvb.at[2 * r + k, q], relay_send.at[r, q], kv_recv.at[2 * r + k, q], other_dp, line + 14 + k
        )

    def passes_on(b):
        gap = jnp.logical_or(jnp.logical_and(b == 0, c >= 4), jnp.logical_and(b == 1, c >= 6))
        return jnp.logical_and(c < 7, jnp.logical_not(gap))

    def passes_back(b):
        return jnp.logical_and(b == 0, c >= 6)

    def send_own(q):
        @pl.when(c < 7)
        def _():
            ring_copy(c, q).start()

        @pl.when(c == 0)
        def _():
            rev_copy(q).start()

        sib_copy(c, q).start()

    gk.sib_recv(oz, 1)
    keys = (kv_part[0] + project(oz, wk)).astype(BF16)
    for h in range(KV_HEADS):
        kvb[own, h] = keys[:, h * HD : (h + 1) * HD]
        send_own(h)
    gv.sib_recv(oz, 1)
    values = (kv_part[1] + project(oz, wv)).astype(BF16)
    for h in range(KV_HEADS):
        for part in range(2):
            kvb[own, 2 + h, pl.ds(part * 128, 128)] = values[part * 128 : (part + 1) * 128, h * HD : (h + 1) * HD].T
        send_own(2 + h)

    def block_at(s):
        last = -4 * least(s, 3) + 5 * least(s, 4) - least(s, 6) + 2 * least(s, 7)
        before = -2 * least(s, 4) + 3 * least(s, 5)
        return c - s + last * least(c, 7) + before * (least(c, 6) - least(c, 7))

    def forward(s, j):
        b = block_at(s)

        @pl.when(s <= c)
        def _():
            for q in (2 * j, 2 * j + 1):
                kv_wait(2 * b + k, q)

                @pl.when(passes_on(b))
                def _():
                    ring_copy(b, q).start()

                @pl.when(passes_back(b))
                def _():
                    back_copy(b, q).start()

                sib_copy(b, q).start()

    def relay_on(r, j):
        @pl.when(c == 4)
        def _():
            for q in (2 * j, 2 * j + 1):
                ref = relay.at[r, q]
                remote(ref, ref, rev_send.at[q], relay_recv.at[r, q], dp, ctx).wait_recv()
                relay_copy(r, q).start()

    def attend(b, h, diag):
        kp = jnp.concatenate([kvb[2 * b, h], kvb[2 * b + 1, h]], axis=0)
        v0, v1 = kvb[2 * b, 2 + h], kvb[2 * b + 1, 2 + h]
        vt = jnp.concatenate([v0[:128], v0[128:], v1[:128], v1[128:]], axis=1)
        queries = jnp.concatenate([qt[h, g] for g in range(GROUPS)], axis=1)
        wide = jnp.dot(kp, queries, preferred_element_type=F32) * (SCALE * LOG2E)
        for g in range(GROUPS):
            i = h * GROUPS + g
            s = wide[:, g * ROWS : (g + 1) * ROWS]
            if diag:
                key = lax.broadcasted_iota(jnp.int32, (2 * ROWS, ROWS), 0)
                row = lax.broadcasted_iota(jnp.int32, (2 * ROWS, ROWS), 1)
                s = jnp.where(key <= k * ROWS + row, s, BIG)
            best = jnp.max(s, axis=0, keepdims=True)
            if not diag:
                old = m_ref[i]
                best = jnp.maximum(old, best)
                carry = jnp.exp2(old - best)
            p = jnp.exp2(s - best)
            total = jnp.sum(p, axis=0, keepdims=True)
            out = jnp.dot(vt, p.astype(BF16), preferred_element_type=F32)
            m_ref[i] = best
            if diag:
                l_ref[i] = total
                acc_ref[i] = out
            else:
                l_ref[i] = l_ref[i] * carry + total
                acc_ref[i] = acc_ref[i] * carry + out

    gq.own_mid()
    gq.other_recv()
    gq.y_start()
    go.z_start()
    slot_row = lax.broadcasted_iota(jnp.int32, (4, 2048), 0) == y
    own_q = jnp.sum(jnp.where(slot_row, tq_ref[...].astype(F32), 0.0), axis=0, keepdims=True)
    head_of = lax.broadcasted_iota(jnp.int32, (T_HEADS, 2048), 1) // HD
    diagonal = head_of == lax.broadcasted_iota(jnp.int32, (T_HEADS, 2048), 0)
    q_heads = jnp.where(diagonal, own_q, 0.0).astype(BF16)
    locals_[1].wait()
    ts = lax.dot_general(q_heads, tk[...], (((1,), (1,)), ((), ())), preferred_element_type=F32) * SCALE
    t_valid = pos * ROWS + lax.broadcasted_iota(jnp.int32, (T_HEADS, ROWS), 1) < length
    ts = jnp.where(t_valid, ts, BIG)
    t_best = jnp.max(ts, axis=1, keepdims=True)
    t_weights = jnp.where(t_valid, jnp.exp(ts - t_best), 0.0)
    t_total = jnp.sum(t_weights, axis=1, keepdims=True)
    locals_[2].wait()
    t_out = jnp.dot(t_weights.astype(BF16), tv[...], preferred_element_type=F32)
    t_sum = jnp.sum(jnp.where(diagonal, t_out * thead_ref[...], 0.0), axis=1, keepdims=True)
    eye = lax.broadcasted_iota(jnp.int32, (T_HEADS, 128), 0) == lax.broadcasted_iota(jnp.int32, (T_HEADS, 128), 1)

    def row_of(column):
        return jnp.sum(jnp.where(eye, column, 0.0), axis=0, keepdims=True)

    tsib[k] = jnp.concatenate([row_of(t_best), row_of(t_total), row_of(t_sum)], axis=1)

    def t_copy():
        return remote(tsib.at[k], tsib.at[k], t_send.at[0], t_recv.at[0], dp, sib_ctx)

    def merged(rows):
        best = jnp.max(rows[:, :128], axis=0, keepdims=True)
        factor = jnp.exp(rows[:, :128] - best)
        sums = [jnp.sum(rows[:, n : n + 128] * factor, axis=0, keepdims=True) for n in (128, 256)]
        return jnp.concatenate([best] + sums, axis=1)

    def t_gather():
        return remote(tbuf.at[c], tbuf.at[c], t_send.at[1], t_recv.at[1 + c], dp, line + 12 + k)

    t_copy().start()

    gq.own_recv()
    locals_[5].wait()
    gq.sib_copy(zh, 0).start()
    go.own_start()
    forward(1, 0)
    relay_on(0, 0)
    gq.y_mid()
    forward(1, 1)
    relay_on(0, 1)

    @pl.when(c == 1)
    def _():
        for q in range(4):
            rev_copy(q).start()

    go.z_recv()
    go.other_start()
    gq.y_recv()
    gq.sib_copy(oz, 1).start()
    forward(2, 0)
    gq.sib_recv(zh, 0)
    gq.sib_recv(oz, 1)
    query = jnp.dot(hid[...], wq[...].reshape(D, HEADS * HD), preferred_element_type=F32).astype(BF16)
    for i in range(HEADS):
        qt[i // GROUPS, i % GROUPS] = query[:, i * HD : (i + 1) * HD].T
    forward(2, 1)
    remote(tsib.at[1 - k], tsib.at[1 - k], t_send.at[0], t_recv.at[0], dp, ctx).wait_recv()
    tbuf[c] = merged(jnp.concatenate([tsib[0], tsib[1]], axis=0))

    @pl.when(c != 6)
    def _():
        t_gather().start()

    go.own_mid()
    for h in range(KV_HEADS):
        for q in (h, 2 + h):
            kv_wait(2 * c + 1 - k, q)
        attend(c, h, True)
    go.other_recv()
    go.y_start()

    def first_part(u):
        return u - 1 - (9 - u) * (1 - (u + 7) // 16)

    def part(a, carry):
        pair, h = a // 2, a % 2

        @pl.when(pair <= c)
        def _():
            b = block_at(pair)
            for j in range(2):
                kv_wait(2 * b + 1 - k, 2 * j + h)
            attend(b, h, False)

        return carry

    def step(s, carry):
        for j in range(2):
            forward(s, j)

            @pl.when(s == 3)
            def _():
                relay_on(1, j)

            u = 2 * s + j
            lax.fori_loop(first_part(u), first_part(u + 1), part, 0)

        @pl.when(s == 3)
        def _():
            go.own_recv()
            locals_[6].wait()
            go.sib_copy(zh, 0).start()

        @pl.when(s == 4)
        def _():
            go.y_mid()

        @pl.when(s == 5)
        def _():
            go.y_recv()
            go.sib_copy(oz, 1).start()

        return carry

    lax.fori_loop(3, 8, step, 0)
    part(15, 0)

    for i in range(HEADS):
        att[:, i * HD : (i + 1) * HD] = (acc_ref[i] / l_ref[i]).astype(BF16).T
    go.sib_recv(zh, 0)
    go.sib_recv(oz, 1)
    hidden = hid[...].astype(F32) + jnp.dot(att[...], wo[...].reshape(D, D), preferred_element_type=F32)
    valid = pos * ROWS + lax.broadcasted_iota(jnp.int32, (ROWS, 1), 0) < length
    rate = jnp.where(valid, lax.rsqrt(jnp.mean(hidden * hidden, axis=1, keepdims=True) + 1e-05), 0.0)
    part = jnp.sum(hidden * rate, axis=0, keepdims=True) * gain_ref[...]
    out_ref[...] = jnp.where(valid, hidden, 0.0)

    def chain_copy():
        return remote(cstage, cbuf.at[c], c_send, c_recv.at[c], dp, line + 12 + k)

    cstage[...] = part

    @pl.when(c <= 5)
    def _():
        chain_copy().start()

    root = 2 * (c - 6) + k
    lanes = lax.broadcasted_iota(jnp.int32, (1, 128), 1)

    @pl.when(c == 7)
    def _():
        trow[...] = jnp.zeros_like(trow)

    @pl.when(c == 6)
    def _():
        for i in (0, 1, 2, 3, 4, 5, 7):
            remote(tbuf.at[i], tbuf.at[i], t_send.at[0], t_recv.at[1 + i], dp, ctx).wait_recv()
        stats = merged(tbuf[...].reshape(8, 384))
        in_heads = lanes < T_HEADS
        above, below = stats[:, 256:], jnp.where(in_heads, stats[:, 128:256], 1.0)
        t_score = jnp.sum(jnp.where(in_heads, above / below, 0.0), axis=1, keepdims=True)
        trow[...] = jnp.where(k == 0, jnp.broadcast_to(t_score, (1, 128)), 0.0)
        for i in range(6):
            remote(cstage, cbuf.at[i], c_send, c_recv.at[i], dp, ctx).wait_recv()
        cstage[...] = cstage[...] + jnp.sum(cbuf[...].reshape(6, D), axis=0, keepdims=True)

    def p_copy(d):
        return remote(pbuf.at[root], pbuf.at[root], p_send.at[d], p_recv.at[root], dp, line + (pos + d) % 16)

    spot = 4 * x + y

    def r_copy(d):
        there = (spot + d) % 16
        return remote(
            rbuf.at[spot], rbuf.at[spot], r_send.at[d], r_recv.at[d], 2 * (there // 4) + zh, 16 * (there % 4) + pos
        )

    deep = 16 * zh + pos

    def s_copy(d):
        there = (deep + d) % 32
        slot = sbuf.at[4 * zh + root]
        return remote(slot, slot, s_send.at[d], s_recv.at[4 * zh + root], 2 * x + there // 16, line + there % 16)

    @pl.when(c >= 6)
    def _():
        mean = cstage[...] / length.astype(F32)
        student = jnp.sum(mean * shead_ref[...], axis=1, keepdims=True)
        rbuf[spot] = jnp.where(lanes == thread, student, 0.0) + jnp.where(lanes == 64 + thread, trow[...], 0.0)
        for d in range(1, 16):
            r_copy(d).start()
        pbuf[root] = jnp.concatenate([mean, trow[...]], axis=1)
        for d in range(1, 16):
            p_copy(d).start()
        for d in range(1, 16):
            ref = rbuf.at[(spot + 16 - d) % 16]
            remote(ref, ref, r_send.at[0], r_recv.at[d], dp, ctx).wait_recv()
        sbuf[4 * zh + root] = jnp.sum(rbuf[...].reshape(16, 128), axis=0, keepdims=True)
        for d in range(1, 32):
            s_copy(d).start()

    for r in range(4):

        @pl.when(pos != 12 + r)
        def _():
            ref = pbuf.at[r]
            remote(ref, ref, p_send.at[0], p_recv.at[r], dp, ctx).wait_recv()

    ybuf[y] = (pbuf[0] + pbuf[1]) + (pbuf[2] + pbuf[3])

    def y_copy(d):
        return remote(ybuf.at[y], ybuf.at[y], y_send.at[d], y_recv.at[d], dp, y_peer(d))

    for d in range(1, 4):
        y_copy(d).start()

    def sent(b, carry):
        for q in range(4):

            @pl.when(jnp.logical_or(passes_on(b), passes_back(b)))
            def _():
                ring_copy(b, q).wait_send()

            sib_copy(b, q).wait_send()
        return carry

    lax.fori_loop(0, c + 1, sent, 0)

    @pl.when(c <= 1)
    def _():
        for q in range(4):
            rev_copy(q).wait_send()

    @pl.when(c == 4)
    def _():
        for r in range(2):
            for q in range(4):
                relay_copy(r, q).wait_send()

    for gather in (gk, gv, gq, go):
        gather.finish()
    t_copy().wait_send()

    @pl.when(c != 6)
    def _():
        t_gather().wait_send()

    @pl.when(c <= 5)
    def _():
        chain_copy().wait_send()

    @pl.when(c >= 6)
    def _():
        for d in range(1, 16):
            r_copy(d).wait_send()
            p_copy(d).wait_send()

    for d in range(1, 4):
        ref = ybuf.at[(y + 4 - d) % 4]
        remote(ref, ref, y_send.at[0], y_recv.at[d], dp, ctx).wait_recv()
    rows = jnp.concatenate([ybuf[i] for i in range(4)], axis=0)
    pooled_ref[...] = rows[:, :D]
    eye4 = lax.broadcasted_iota(jnp.int32, (4, 4), 0) == lax.broadcasted_iota(jnp.int32, (4, 4), 1)
    tscore_ref[...] = jnp.sum(jnp.where(eye4, rows[:, D : D + 4], 0.0), axis=0, keepdims=True)
    for d in range(1, 4):
        y_copy(d).wait_send()

    for r in range(8):

        @pl.when(deep != 12 + r + 12 * (r // 4))
        def _():
            ref = sbuf.at[r]
            remote(ref, ref, s_send.at[0], s_recv.at[r], dp, ctx).wait_recv()

    every = jnp.sum(sbuf[...].reshape(8, 128), axis=0, keepdims=True)
    threads = list_ref.shape[1]
    student_all, teacher_all = every[:, :threads], every[:, 64 : 64 + threads]
    target = teacher_all + rel_ref[...].astype(F32)
    member = lax.broadcasted_iota(jnp.int32, (8, threads), 0) == list_ref[...]

    def log_soft(logits):
        masked = jnp.where(member, logits, BIG)
        top = jnp.max(masked, axis=1, keepdims=True)
        shifted = jnp.where(member, jnp.exp(masked - top), 0.0)
        return masked - top - jnp.log(jnp.sum(shifted, axis=1, keepdims=True))

    target_log = log_soft(target)
    student_log = log_soft(student_all)
    target_prob = jnp.where(member, jnp.exp(target_log), 0.0)
    terms = jnp.where(member, target_prob * (target_log - student_log), 0.0)
    div_column = jnp.sum(terms, axis=1, keepdims=True)
    eye8 = lax.broadcasted_iota(jnp.int32, (8, 8), 0) == lax.broadcasted_iota(jnp.int32, (8, 8), 1)
    div_ref[...] = jnp.sum(jnp.where(eye8, div_column, 0.0), axis=0, keepdims=True)

    @pl.when(c >= 6)
    def _():
        for d in range(1, 32):
            s_copy(d).wait_send()


def place(out, pooled, tscore, div, out_ref, pooled_ref, tscore_ref, div_ref):
    out_ref[...] = out[...]
    pooled_ref[...] = pooled[...]
    tscore_ref[...] = tscore[...]
    div_ref[...] = div[...]


def local(
    student_hidden, w_query, w_keyval, w_out, norm_gain, student_head, teacher_query, teacher_keys, teacher_values,
    teacher_head, thread_lengths, list_index, relevance,
):
    vmem = pl.BlockSpec(memory_space=pltpu.VMEM)
    anywhere = pl.BlockSpec(memory_space=pl.ANY)
    dma = pltpu.SemaphoreType.DMA
    out, pooled, tscore, div = pl.pallas_call(
        kernel,
        out_shape=(
            jax.ShapeDtypeStruct((ROWS, D), F32),
            jax.ShapeDtypeStruct((4, D), F32),
            jax.ShapeDtypeStruct((1, 4), F32),
            jax.ShapeDtypeStruct((1, 8), F32),
        ),
        in_specs=[anywhere] * 13,
        out_specs=(vmem,) * 4,
        scratch_shapes=[
            pltpu.VMEM((ROWS, D), BF16),
            pltpu.VMEM((4, 2, 128, 256), BF16),
            pltpu.VMEM((4, 2, 128, 256), BF16),
            pltpu.VMEM((4, 2, 128, D), BF16),
            pltpu.VMEM((4, 2, 128, D), BF16),
            pltpu.VMEM((ROWS, 2048), BF16),
            pltpu.VMEM((ROWS, 2048), BF16),
            pltpu.VMEM((16, 4, 256, 128), BF16),
            pltpu.VMEM((2, 4, 256, 128), BF16),
            pltpu.VMEM((KV_HEADS, GROUPS, HD, ROWS), BF16),
            pltpu.VMEM((ROWS, D), BF16),
            pltpu.VMEM((HEADS, 1, ROWS), F32),
            pltpu.VMEM((HEADS, 1, ROWS), F32),
            pltpu.VMEM((HEADS, HD, ROWS), F32),
            pltpu.VMEM((2, 1, 384), F32),
            pltpu.VMEM((8, 1, 384), F32),
            pltpu.VMEM((1, 128), F32),
            pltpu.VMEM((6, 1, D), F32),
            pltpu.VMEM((1, D), F32),
            pltpu.VMEM((4, 1, D + 128), F32),
            pltpu.VMEM((16, 1, 128), F32),
            pltpu.VMEM((4, 1, D + 128), F32),
            pltpu.VMEM((8, 1, 128), F32),
            pltpu.VMEM((2, ROWS, 256), F32),
            pltpu.VMEM((1, D), F32),
            pltpu.VMEM((1, D), F32),
            pltpu.VMEM((4, 2048), BF16),
            pltpu.VMEM((1, 2048), F32),
            pltpu.SMEM((32,), jnp.int32),
            pltpu.VMEM((1, 32), jnp.int32),
            pltpu.VMEM((1, 32), jnp.int32),
            dma((14,)),
            dma((4, 17)),
            dma((4, 14)),
            dma((16, 4)),
            dma((8, 4)),
            dma((8, 4)),
            dma((4,)),
            dma((2, 4)),
            dma((2, 4)),
            dma((2,)),
            dma((9,)),
            dma,
            dma((6,)),
            dma((16,)),
            dma((4,)),
            dma((16,)),
            dma((16,)),
            dma((4,)),
            dma((4,)),
            dma((32,)),
            dma((8,)),
        ],
        compiler_params=pltpu.CompilerParams(
            collective_id=0, has_side_effects=True, vmem_limit_bytes=60 * 1024 * 1024
        ),
        cost_estimate=pl.CostEstimate(flops=10**10, bytes_accessed=8 * 2**20, transcendentals=8 * 10**6),
    )(
        student_hidden, w_keyval, w_query, w_out, norm_gain.reshape(1, -1), student_head.reshape(1, -1), teacher_query,
        teacher_keys, teacher_values, teacher_head.reshape(1, -1), thread_lengths, list_index.reshape(1, -1),
        relevance.reshape(1, -1),
    )
    out, pooled, tscore, div = pl.pallas_call(
        place,
        out_shape=tuple(jax.ShapeDtypeStruct(a.shape, a.dtype) for a in (out, pooled, tscore, div)),
        in_specs=[vmem] * 4,
        out_specs=(vmem,) * 4,
        compiler_params=pltpu.CompilerParams(vmem_limit_bytes=60 * 1024 * 1024),
    )(out, pooled, tscore, div)
    return out, pooled, tscore.reshape(4), div.reshape(8)


def solution(mesh):
    return jax.shard_map(
        local,
        mesh=mesh,
        in_specs=(
            P(("dp", "ctx"), None), P("dp", None), P("dp", None), P("dp", None), P(), P(), P("dp", None),
            P(("dp", "ctx"), None), P(("dp", "ctx"), None), P(), P(), P(), P(),
        ),
        out_specs=(P(("dp", "ctx"), None), P("dp", None), P("dp"), P()),
        check_vma=False,
    )
```

time: 99.9 us -> 88.4 us (0.88)
  Pallas kernels: 99.1 us -> 87.6 us
    pallas_call x1, Pallas kernels: 96.8 us -> 85.3 us  [local(): pl.pallas_call(kernel, out_shape=(jax.ShapeDtypeStruct((ROWS, D), F32), j...]
where the time goes in v3:
time: 88.4 us; the launch traced here: 88.2 us
  Pallas kernels  87.6 us (99%)
    pallas_call x1, Pallas kernels, local(): pl.pallas_call(kernel, out_shape=(jax.ShapeDtypeStruct((ROWS, D), F32), j...  85.3 us
    pallas_call x1, Pallas kernels, local(): pl.pallas_call(place, out_shape=tuple((jax.ShapeDtypeStruct(a.shape, a.dt...  2.29 us

profile of v3, /device:TPU:1, one launch (start us, length us, event | category | flops | bytes accessed | tf_op | source)
XLA Modules:
  0.0 88.2 jit_solution(3051247586039099281)
XLA Ops:
  0.6 85.3 %shard_map.156 = (f32[256,1024]{1,0:T(8,128)}, f32[4,1024]{1,0:T(4,128)}, f32[1,4]{1,0:T(1,128)}, f32[1,8]{1,0:T(1,128)}) custom-call(bf16[256,1024]{1,0:T(8,128)(2,1)} %hid_in.1, bf16[128,512]{1,0:T(8,128)(2,1)} %wkv_in.1, bf16[128,1024]{1,0:T(8,128)(2,1)} %wq_in.1, bf16[128,1024]{1,0:T(8,128)(2,1)} %wo_in.1, f32[1,1024]{1,0:T(1,128)} %bitcast.8, ...), custom_call_target="tpu_custom_call" | custom-call | flops 10000000000 | bytes 8388608 | tf_op jit(solution)/shard_map/pallas_call | solution.py:745
  85.9 2.3 %shard_map.157 = (f32[256,1024]{1,0:T(8,128)}, f32[4,1024]{1,0:T(4,128)}, f32[1,4]{1,0:T(1,128)}, f32[1,8]{1,0:T(1,128)}) custom-call(f32[256,1024]{1,0:T(8,128)} %get-tuple-element.12.out, f32[4,1024]{1,0:T(4,128)} %get-tuple-element.13.pooled, f32[1,4]{1,0:T(1,128)} %get-tuple-element.14.tscore, f32[1,8]{1,0:T(1,128)} %get-tuple-element.15.div), custom_call_target="tpu_custom_call" | custom-call | tf_op jit(solution)/shard_map/pallas_call | solution.py:818

commit v4 on v3

--- a/solution.py
+++ b/solution.py
@@ -136,7 +136,7 @@
             self.i = i
             self.w_in, self.w = weights[i]
             self.piece = 64 * k + 16 * y
-            self.ring = i >= 2
+            self.ring, self.fine = i >= 2, i == 0
 
         def sem(self, table, n):
             return table.at[self.i, n]
@@ -212,8 +212,7 @@
 
         def other_recv(self):
             for d in range(1, 4):
-                w = self.w.at[(x + 4 - d) % 4, oz, pl.ds(self.piece, 16)]
-                remote(w, w, self.sem(wsend, 0), self.sem(wrecv, 3 + d), dp, ctx).wait_recv()
+                self.arrived(self.w.at[(x + 4 - d) % 4, oz, pl.ds(self.piece, 16)], 3 + d)
 
         def y_part(self, at, first=0, count=4):
             return self.w.at[pl.ds(first, count), oz, pl.ds(64 * k + 16 * ((y + at) % 4), 16)]
@@ -229,6 +228,26 @@
                 remote(left, left, self.sem(wsend, 11), self.sem(wrecv, 8), dp, y_peer(1)),
                 remote(right, right, self.sem(wsend, 16), self.sem(wrecv, 13), dp, y_peer(3)),
             ]
+
+        def fine_copy(self, at, d):
+            w = self.w.at[(x + at) % 4, oz, pl.ds(self.piece, 16)]
+            n = 3 * at + d
+            return remote(w, w, self.sem(wsend, 16 + n), self.sem(wrecv, 13 + n), dp, y_peer(d))
+
+        def fine_start(self, at):
+            for d in range(1, 4):
+                self.fine_copy(at, d).start()
+
+        def fine_rest(self):
+            for d in (1, 3, 2):
+                self.arrived(self.w.at[(x + 4 - d) % 4, oz, pl.ds(self.piece, 16)], 3 + d)
+                self.fine_start(4 - d)
+
+        def fine_recv(self):
+            for at in range(4):
+                for d in range(1, 4):
+                    w = self.w.at[(x + at) % 4, oz, pl.ds(64 * k + 16 * ((y + 4 - d) % 4), 16)]
+                    self.arrived(w, 13 + 3 * at + d)
 
         def y_start(self):
             for copy in self.y_copies():
@@ -268,7 +287,11 @@
                 for j in range(4):
                     self.z_copy(j).wait_send()
 
-            copies = self.own_copies() + self.y_copies() + [self.other_copy(d) for d in range(1, 4)]
+            copies = self.own_copies() + [self.other_copy(d) for d in range(1, 4)]
+            if self.fine:
+                copies += [self.fine_copy(at, d) for at in range(4) for d in range(1, 4)]
+            else:
+                copies += self.y_copies()
             for copy in copies + (self.own_relays() + self.y_relays() if self.ring else []):
                 copy.wait_send()
             self.sib_copy(zh, 0).wait_send()
@@ -279,20 +302,26 @@
     length = len_ref[thread]
     gk, gv, gq, go = (Gather(i) for i in range(4))
 
-    for gather in (gk, gv):
-        gather.z_start()
-        gather.own_start()
-    for gather in (gk, gv):
-        gather.z_recv()
-        gather.other_start()
+    gk.z_start()
+    gk.own_start()
+    gv.z_start()
+    gk.z_recv()
+    gk.other_start()
+    gk.fine_start(0)
+    gv.own_start()
+    gv.z_recv()
+    gv.other_start()
     gq.z_start()
-    for gather, copy in ((gk, locals_[3]), (gv, locals_[4])):
-        gather.own_recv()
-        copy.wait()
-        gather.sib_copy(zh, 0).start()
-    for gather in (gk, gv):
-        gather.other_recv()
-        gather.y_start()
+    go.z_start()
+    gk.own_recv()
+    locals_[3].wait()
+    gk.sib_copy(zh, 0).start()
+    gk.fine_rest()
+    gv.other_recv()
+    gv.y_start()
+    gv.own_recv()
+    locals_[4].wait()
+    gv.sib_copy(zh, 0).start()
     gq.own_start()
     locals_[0].wait()
 
@@ -302,13 +331,12 @@
 
     gk.sib_recv(zh, 0)
     kv_part[0] = project(zh, wk)
+    gq.z_recv()
+    gq.other_start()
+    gk.fine_recv()
+    gk.sib_copy(oz, 1).start()
     gv.sib_recv(zh, 0)
     kv_part[1] = project(zh, wv)
-    for gather in (gk, gv):
-        gather.y_recv()
-        gather.sib_copy(oz, 1).start()
-    gq.z_recv()
-    gq.other_start()
     own = 2 * c + k
 
     def hand(b, q, ssem, to_ctx):
@@ -361,6 +389,8 @@
     for h in range(KV_HEADS):
         kvb[own, h] = keys[:, h * HD : (h + 1) * HD]
         send_own(h)
+    gv.y_recv()
+    gv.sib_copy(oz, 1).start()
     gv.sib_recv(oz, 1)
     values = (kv_part[1] + project(oz, wv)).astype(BF16)
     for h in range(KV_HEADS):
@@ -431,7 +461,6 @@
     gq.own_mid()
     gq.other_recv()
     gq.y_start()
-    go.z_start()
     slot_row = lax.broadcasted_iota(jnp.int32, (4, 2048), 0) == y
     own_q = jnp.sum(jnp.where(slot_row, tq_ref[...].astype(F32), 0.0), axis=0, keepdims=True)
     head_of = lax.broadcasted_iota(jnp.int32, (T_HEADS, 2048), 1) // HD
@@ -617,7 +646,7 @@
         mean = cstage[...] / length.astype(F32)
         student = jnp.sum(mean * shead_ref[...], axis=1, keepdims=True)
         rbuf[spot] = jnp.where(lanes == thread, student, 0.0) + jnp.where(lanes == 64 + thread, trow[...], 0.0)
-        for d in range(1, 16):
+        for d in sorted(range(1, 16), key=lambda d: -min(d // 4, 4 - d // 4) - min(d % 4, 4 - d % 4)):
             r_copy(d).start()
         pbuf[root] = jnp.concatenate([mean, trow[...]], axis=1)
         for d in range(1, 16):
@@ -626,7 +655,7 @@
             ref = rbuf.at[(spot + 16 - d) % 16]
             remote(ref, ref, r_send.at[0], r_recv.at[d], dp, ctx).wait_recv()
         sbuf[4 * zh + root] = jnp.sum(rbuf[...].reshape(16, 128), axis=0, keepdims=True)
-        for d in range(1, 32):
+        for d in sorted(range(1, 32), key=lambda d: abs(d - 16)):
             s_copy(d).start()
 
     for r in range(4):
@@ -728,11 +757,14 @@
             s_copy(d).wait_send()
 
 
-def place(out, pooled, tscore, div, out_ref, pooled_ref, tscore_ref, div_ref):
-    out_ref[...] = out[...]
-    pooled_ref[...] = pooled[...]
-    tscore_ref[...] = tscore[...]
-    div_ref[...] = div[...]
+def place(*refs):
+    sems = refs[-1]
+    half = (len(refs) - 1) // 2
+    copies = [pltpu.make_async_copy(refs[i], refs[half + i], sems.at[i]) for i in range(half)]
+    for copy in copies:
+        copy.start()
+    for copy in copies:
+        copy.wait()
 
 
 def local(
@@ -745,10 +777,10 @@
     out, pooled, tscore, div = pl.pallas_call(
         kernel,
         out_shape=(
-            jax.ShapeDtypeStruct((ROWS, D), F32),
-            jax.ShapeDtypeStruct((4, D), F32),
-            jax.ShapeDtypeStruct((1, 4), F32),
-            jax.ShapeDtypeStruct((1, 8), F32),
+            pltpu.VMEM((ROWS, D), F32),
+            pltpu.VMEM((4, D), F32),
+            pltpu.VMEM((1, 4), F32),
+            pltpu.VMEM((1, 8), F32),
         ),
         in_specs=[anywhere] * 13,
         out_specs=(vmem,) * 4,
@@ -785,8 +817,8 @@
             pltpu.VMEM((1, 32), jnp.int32),
             pltpu.VMEM((1, 32), jnp.int32),
             dma((14,)),
-            dma((4, 17)),
-            dma((4, 14)),
+            dma((4, 29)),
+            dma((4, 26)),
             dma((16, 4)),
             dma((8, 4)),
             dma((8, 4)),
@@ -819,8 +851,9 @@
         place,
         out_shape=tuple(jax.ShapeDtypeStruct(a.shape, a.dtype) for a in (out, pooled, tscore, div)),
         in_specs=[vmem] * 4,
-        out_specs=(vmem,) * 4,
-        compiler_params=pltpu.CompilerParams(vmem_limit_bytes=60 * 1024 * 1024),
+        out_specs=(anywhere,) * 4,
+        scratch_shapes=[dma((4,))],
+        compiler_params=pltpu.CompilerParams(vmem_limit_bytes=16 * 1024 * 1024),
     )(out, pooled, tscore, div)
     return out, pooled, tscore.reshape(4), div.reshape(8)
 

time: 88.4 us -> 84.3 us (0.954)
  Pallas kernels: 87.6 us -> 83.5 us
    pallas_call x1, Pallas kernels: 85.3 us -> 82.5 us  [local(): pl.pallas_call(kernel, out_shape=(pltpu.VMEM((ROWS, D), F32), pltpu.VMEM(...]
    pallas_call x1, Pallas kernels: 2.29 us -> 1.01 us  [local(): pl.pallas_call(place, out_shape=tuple((jax.ShapeDtypeStruct(a.shape, a.dt...]
where the time goes in v4:
time: 84.3 us; the launch traced here: 84.1 us
  Pallas kernels  83.5 us (99%)
    pallas_call x1, Pallas kernels, local(): pl.pallas_call(kernel, out_shape=(pltpu.VMEM((ROWS, D), F32), pltpu.VMEM(...  82.5 us

profile of v4, /device:TPU:1, one launch (start us, length us, event | category | flops | bytes accessed | tf_op | source)
XLA Modules:
  0.0 84.1 jit_solution(6971982730130951994)
XLA Ops:
  0.6 82.5 %shard_map.156 = (f32[256,1024]{1,0:T(8,128)S(1)}, f32[4,1024]{1,0:T(4,128)S(1)}, f32[1,4]{1,0:T(1,128)S(1)}, f32[1,8]{1,0:T(1,128)S(1)}) custom-call(bf16[256,1024]{1,0:T(8,128)(2,1)} %hid_in.1, bf16[128,512]{1,0:T(8,128)(2,1)} %wkv_in.1, bf16[128,1024]{1,0:T(8,128)(2,1)} %wq_in.1, bf16[128,1024]{1,0:T(8,128)(2,1)} %wo_in.1, f32[1,1024]{1,0:T(1,128)} %bitcast.8, ...), custom_call_target="tpu_custom_call" | custom-call | flops 10000000000 | bytes 8388608 | tf_op jit(solution)/shard_map/pallas_call | solution.py:777
  83.1 1.0 %shard_map.157 = (f32[256,1024]{1,0:T(8,128)}, f32[4,1024]{1,0:T(4,128)}, f32[1,4]{1,0:T(1,128)}, f32[1,8]{1,0:T(1,128)}) custom-call(f32[256,1024]{1,0:T(8,128)S(1)} %get-tuple-element.12.refs_0_, f32[4,1024]{1,0:T(4,128)S(1)} %get-tuple-element.13.refs_1_, f32[1,4]{1,0:T(1,128)S(1)} %get-tuple-element.14.refs_2_, f32[1,8]{1,0:T(1,128)S(1)} %get-tuple-element.15.refs_3_), custom_call_target="tpu_custom_call" | custom-call | tf_op jit(solution)/shard_map/pallas_call | solution.py:850

commit v5 on v4

--- a/solution.py
+++ b/solution.py
@@ -26,10 +26,10 @@
 def kernel(
     hid_in, wkv_in, wq_in, wo_in, gain_in, shead_in, tq_in, tk_in, tv_in, thead_in, len_in, list_in, rel_in,
     out_ref, pooled_ref, tscore_ref, div_ref,
-    hid, wk, wv, wq, wo, tk, tv, kvb, relay, qt, att, m_ref, l_ref, acc_ref,
+    hid, hidp, wk, wv, wq, wo, tk, tv, kvb, relay, qt, att, m_ref, l_ref, acc_ref,
     tsib, tbuf, trow, cbuf, cstage, pbuf, rbuf, ybuf, sbuf, kv_part,
     gain_ref, shead_ref, tq_ref, thead_ref, len_ref, list_ref, rel_ref,
-    lsem, wsend, wrecv, kv_recv, kv_send, sib_send, rev_send, relay_recv, relay_send,
+    lsem, hsem, wsend, wrecv, kv_recv, kv_send, sib_send, rev_send, relay_recv, relay_send,
     t_send, t_recv, c_send, c_recv, p_send, p_recv, r_send, r_recv, y_send, y_recv, s_send, s_recv,
 ):
     dp = lax.axis_index("dp")
@@ -136,7 +136,7 @@
             self.i = i
             self.w_in, self.w = weights[i]
             self.piece = 64 * k + 16 * y
-            self.ring, self.fine = i >= 2, i == 0
+            self.ring = i >= 2
 
         def sem(self, table, n):
             return table.at[self.i, n]
@@ -229,26 +229,6 @@
                 remote(right, right, self.sem(wsend, 16), self.sem(wrecv, 13), dp, y_peer(3)),
             ]
 
-        def fine_copy(self, at, d):
-            w = self.w.at[(x + at) % 4, oz, pl.ds(self.piece, 16)]
-            n = 3 * at + d
-            return remote(w, w, self.sem(wsend, 16 + n), self.sem(wrecv, 13 + n), dp, y_peer(d))
-
-        def fine_start(self, at):
-            for d in range(1, 4):
-                self.fine_copy(at, d).start()
-
-        def fine_rest(self):
-            for d in (1, 3, 2):
-                self.arrived(self.w.at[(x + 4 - d) % 4, oz, pl.ds(self.piece, 16)], 3 + d)
-                self.fine_start(4 - d)
-
-        def fine_recv(self):
-            for at in range(4):
-                for d in range(1, 4):
-                    w = self.w.at[(x + at) % 4, oz, pl.ds(64 * k + 16 * ((y + 4 - d) % 4), 16)]
-                    self.arrived(w, 13 + 3 * at + d)
-
         def y_start(self):
             for copy in self.y_copies():
                 copy.start()
@@ -288,10 +268,7 @@
                     self.z_copy(j).wait_send()
 
             copies = self.own_copies() + [self.other_copy(d) for d in range(1, 4)]
-            if self.fine:
-                copies += [self.fine_copy(at, d) for at in range(4) for d in range(1, 4)]
-            else:
-                copies += self.y_copies()
+            copies += self.y_copies()
             for copy in copies + (self.own_relays() + self.y_relays() if self.ring else []):
                 copy.wait_send()
             self.sib_copy(zh, 0).wait_send()
@@ -305,9 +282,18 @@
     gk.z_start()
     gk.own_start()
     gv.z_start()
+
+    def hid_copy():
+        return remote(hid_in, hidp, hsem.at[0], hsem.at[1], dp, ctx + 2)
+
+    gives = jnp.logical_and(c >= 5, c <= 6)
+
+    @pl.when(gives)
+    def _():
+        hid_copy().start()
+
     gk.z_recv()
     gk.other_start()
-    gk.fine_start(0)
     gv.own_start()
     gv.z_recv()
     gv.other_start()
@@ -316,7 +302,8 @@
     gk.own_recv()
     locals_[3].wait()
     gk.sib_copy(zh, 0).start()
-    gk.fine_rest()
+    gk.other_recv()
+    gk.y_start()
     gv.other_recv()
     gv.y_start()
     gv.own_recv()
@@ -325,18 +312,54 @@
     gq.own_start()
     locals_[0].wait()
 
-    def project(half, w):
-        parts = [hid[:, pl.ds(pl.multiple_of((2 * i + half) * 128, 128), 128)] for i in range(4)]
+    def project(rows, half, w):
+        parts = [rows[:, pl.ds(pl.multiple_of((2 * i + half) * 128, 128), 128)] for i in range(4)]
         return jnp.dot(jnp.concatenate(parts, axis=1), w[:, half].reshape(512, 256), preferred_element_type=F32)
 
     gk.sib_recv(zh, 0)
-    kv_part[0] = project(zh, wk)
+    kv_part[0] = project(hid, zh, wk)
     gq.z_recv()
     gq.other_start()
-    gk.fine_recv()
+    slot_row = lax.broadcasted_iota(jnp.int32, (4, 2048), 0) == y
+    own_q = jnp.sum(jnp.where(slot_row, tq_ref[...].astype(F32), 0.0), axis=0, keepdims=True)
+    head_of = lax.broadcasted_iota(jnp.int32, (T_HEADS, 2048), 1) // HD
+    diagonal = head_of == lax.broadcasted_iota(jnp.int32, (T_HEADS, 2048), 0)
+    q_heads = jnp.where(diagonal, own_q, 0.0).astype(BF16)
+    locals_[1].wait()
+    ts = lax.dot_general(q_heads, tk[...], (((1,), (1,)), ((), ())), preferred_element_type=F32) * SCALE
+    t_valid = pos * ROWS + lax.broadcasted_iota(jnp.int32, (T_HEADS, ROWS), 1) < length
+    ts = jnp.where(t_valid, ts, BIG)
+    t_best = jnp.max(ts, axis=1, keepdims=True)
+    t_weights = jnp.where(t_valid, jnp.exp(ts - t_best), 0.0)
+    t_total = jnp.sum(t_weights, axis=1, keepdims=True)
+    locals_[2].wait()
+    t_out = jnp.dot(t_weights.astype(BF16), tv[...], preferred_element_type=F32)
+    t_sum = jnp.sum(jnp.where(diagonal, t_out * thead_ref[...], 0.0), axis=1, keepdims=True)
+    eye = lax.broadcasted_iota(jnp.int32, (T_HEADS, 128), 0) == lax.broadcasted_iota(jnp.int32, (T_HEADS, 128), 1)
+
+    def row_of(column):
+        return jnp.sum(jnp.where(eye, column, 0.0), axis=0, keepdims=True)
+
+    tsib[k] = jnp.concatenate([row_of(t_best), row_of(t_total), row_of(t_sum)], axis=1)
+
+    def t_copy():
+        return remote(tsib.at[k], tsib.at[k], t_send.at[0], t_recv.at[0], dp, sib_ctx)
+
+    def merged(rows):
+        best = jnp.max(rows[:, :128], axis=0, keepdims=True)
+        factor = jnp.exp(rows[:, :128] - best)
+        sums = [jnp.sum(rows[:, n : n + 128] * factor, axis=0, keepdims=True) for n in (128, 256)]
+        return jnp.concatenate([best] + sums, axis=1)
+
+    def t_gather():
+        return remote(tbuf.at[c], tbuf.at[c], t_send.at[1], t_recv.at[1 + c], dp, line + 12 + k)
+
+    t_copy().start()
+
+    gk.y_recv()
     gk.sib_copy(oz, 1).start()
     gv.sib_recv(zh, 0)
-    kv_part[1] = project(zh, wv)
+    kv_part[1] = project(hid, zh, wv)
     own = 2 * c + k
 
     def hand(b, q, ssem, to_ctx):
@@ -368,13 +391,14 @@
 
     def passes_on(b):
         gap = jnp.logical_or(jnp.logical_and(b == 0, c >= 4), jnp.logical_and(b == 1, c >= 6))
+        gap = jnp.logical_or(gap, jnp.logical_and(b == c, c >= 5))
         return jnp.logical_and(c < 7, jnp.logical_not(gap))
 
     def passes_back(b):
         return jnp.logical_and(b == 0, c >= 6)
 
     def send_own(q):
-        @pl.when(c < 7)
+        @pl.when(c < 5)
         def _():
             ring_copy(c, q).start()
 
@@ -384,19 +408,39 @@
 
         sib_copy(c, q).start()
 
+    def send_before(q):
+        @pl.when(c == 6)
+        def _():
+            ring_copy(c - 1, q).start()
+
+        sib_copy(c - 1, q).start()
+
+    def put_keys(block, keys, send):
+        keys = keys.astype(BF16)
+        for h in range(KV_HEADS):
+            kvb[block, h] = keys[:, h * HD : (h + 1) * HD]
+            send(h)
+
+    def put_values(block, values, send):
+        values = values.astype(BF16)
+        for h in range(KV_HEADS):
+            for part in range(2):
+                piece = values[part * 128 : (part + 1) * 128, h * HD : (h + 1) * HD]
+                kvb[block, 2 + h, pl.ds(part * 128, 128)] = piece.T
+            send(2 + h)
+
     gk.sib_recv(oz, 1)
-    keys = (kv_part[0] + project(oz, wk)).astype(BF16)
-    for h in range(KV_HEADS):
-        kvb[own, h] = keys[:, h * HD : (h + 1) * HD]
-        send_own(h)
+    put_keys(own, kv_part[0] + project(hid, oz, wk), send_own)
     gv.y_recv()
     gv.sib_copy(oz, 1).start()
     gv.sib_recv(oz, 1)
-    values = (kv_part[1] + project(oz, wv)).astype(BF16)
-    for h in range(KV_HEADS):
-        for part in range(2):
-            kvb[own, 2 + h, pl.ds(part * 128, 128)] = values[part * 128 : (part + 1) * 128, h * HD : (h + 1) * HD].T
-        send_own(2 + h)
+    put_values(own, kv_part[1] + project(hid, oz, wv), send_own)
+
+    @pl.when(c >= 6)
+    def _():
+        remote(hidp, hidp, hsem.at[0], hsem.at[1], dp, ctx).wait_recv()
+        put_keys(own - 2, project(hidp, zh, wk) + project(hidp, oz, wk), send_before)
+        put_values(own - 2, project(hidp, zh, wv) + project(hidp, oz, wv), send_before)
 
     def block_at(s):
         last = -4 * least(s, 3) + 5 * least(s, 4) - least(s, 6) + 2 * least(s, 7)
@@ -406,7 +450,7 @@
     def forward(s, j):
         b = block_at(s)
 
-        @pl.when(s <= c)
+        @pl.when(jnp.logical_and(s <= c, s > c // 6))
         def _():
             for q in (2 * j, 2 * j + 1):
                 kv_wait(2 * b + k, q)
@@ -461,42 +505,6 @@
     gq.own_mid()
     gq.other_recv()
     gq.y_start()
-    slot_row = lax.broadcasted_iota(jnp.int32, (4, 2048), 0) == y
-    own_q = jnp.sum(jnp.where(slot_row, tq_ref[...].astype(F32), 0.0), axis=0, keepdims=True)
-    head_of = lax.broadcasted_iota(jnp.int32, (T_HEADS, 2048), 1) // HD
-    diagonal = head_of == lax.broadcasted_iota(jnp.int32, (T_HEADS, 2048), 0)
-    q_heads = jnp.where(diagonal, own_q, 0.0).astype(BF16)
-    locals_[1].wait()
-    ts = lax.dot_general(q_heads, tk[...], (((1,), (1,)), ((), ())), preferred_element_type=F32) * SCALE
-    t_valid = pos * ROWS + lax.broadcasted_iota(jnp.int32, (T_HEADS, ROWS), 1) < length
-    ts = jnp.where(t_valid, ts, BIG)
-    t_best = jnp.max(ts, axis=1, keepdims=True)
-    t_weights = jnp.where(t_valid, jnp.exp(ts - t_best), 0.0)
-    t_total = jnp.sum(t_weights, axis=1, keepdims=True)
-    locals_[2].wait()
-    t_out = jnp.dot(t_weights.astype(BF16), tv[...], preferred_element_type=F32)
-    t_sum = jnp.sum(jnp.where(diagonal, t_out * thead_ref[...], 0.0), axis=1, keepdims=True)
-    eye = lax.broadcasted_iota(jnp.int32, (T_HEADS, 128), 0) == lax.broadcasted_iota(jnp.int32, (T_HEADS, 128), 1)
-
-    def row_of(column):
-        return jnp.sum(jnp.where(eye, column, 0.0), axis=0, keepdims=True)
-
-    tsib[k] = jnp.concatenate([row_of(t_best), row_of(t_total), row_of(t_sum)], axis=1)
-
-    def t_copy():
-        return remote(tsib.at[k], tsib.at[k], t_send.at[0], t_recv.at[0], dp, sib_ctx)
-
-    def merged(rows):
-        best = jnp.max(rows[:, :128], axis=0, keepdims=True)
-        factor = jnp.exp(rows[:, :128] - best)
-        sums = [jnp.sum(rows[:, n : n + 128] * factor, axis=0, keepdims=True) for n in (128, 256)]
-        return jnp.concatenate([best] + sums, axis=1)
-
-    def t_gather():
-        return remote(tbuf.at[c], tbuf.at[c], t_send.at[1], t_recv.at[1 + c], dp, line + 12 + k)
-
-    t_copy().start()
-
     gq.own_recv()
     locals_[5].wait()
     gq.sib_copy(zh, 0).start()
@@ -689,6 +697,10 @@
     def _():
         for q in range(4):
             rev_copy(q).wait_send()
+
+    @pl.when(gives)
+    def _():
+        hid_copy().wait_send()
 
     @pl.when(c == 4)
     def _():
@@ -785,6 +797,7 @@
         in_specs=[anywhere] * 13,
         out_specs=(vmem,) * 4,
         scratch_shapes=[
+            pltpu.VMEM((ROWS, D), BF16),
             pltpu.VMEM((ROWS, D), BF16),
             pltpu.VMEM((4, 2, 128, 256), BF16),
             pltpu.VMEM((4, 2, 128, 256), BF16),
@@ -817,8 +830,9 @@
             pltpu.VMEM((1, 32), jnp.int32),
             pltpu.VMEM((1, 32), jnp.int32),
             dma((14,)),
-            dma((4, 29)),
-            dma((4, 26)),
+            dma((2,)),
+            dma((4, 17)),
+            dma((4, 14)),
             dma((16, 4)),
             dma((8, 4)),
             dma((8, 4)),

time: 84.3 us -> 82.3 us (0.976)
  Pallas kernels: 83.5 us -> 81.5 us
    pallas_call x1, Pallas kernels: 82.5 us -> 80.5 us  [local(): pl.pallas_call(kernel, out_shape=(pltpu.VMEM((ROWS, D), F32), pltpu.VMEM(...]
where the time goes in v5:
time: 82.3 us; the launch traced here: 82.2 us
  Pallas kernels  81.5 us (99%)
    pallas_call x1, Pallas kernels, local(): pl.pallas_call(kernel, out_shape=(pltpu.VMEM((ROWS, D), F32), pltpu.VMEM(...  80.5 us

profile of v5, /device:TPU:1, one launch (start us, length us, event | category | flops | bytes accessed | tf_op | source)
XLA Modules:
  0.0 82.2 jit_solution(9200354702168381276)
XLA Ops:
  0.6 80.5 %shard_map.156 = (f32[256,1024]{1,0:T(8,128)S(1)}, f32[4,1024]{1,0:T(4,128)S(1)}, f32[1,4]{1,0:T(1,128)S(1)}, f32[1,8]{1,0:T(1,128)S(1)}) custom-call(bf16[256,1024]{1,0:T(8,128)(2,1)} %hid_in.1, bf16[128,512]{1,0:T(8,128)(2,1)} %wkv_in.1, bf16[128,1024]{1,0:T(8,128)(2,1)} %wq_in.1, bf16[128,1024]{1,0:T(8,128)(2,1)} %wo_in.1, f32[1,1024]{1,0:T(1,128)} %bitcast.8, ...), custom_call_target="tpu_custom_call" | custom-call | flops 10000000000 | bytes 8388608 | tf_op jit(solution)/shard_map/pallas_call | solution.py:789
  81.2 1.0 %shard_map.157 = (f32[256,1024]{1,0:T(8,128)}, f32[4,1024]{1,0:T(4,128)}, f32[1,4]{1,0:T(1,128)}, f32[1,8]{1,0:T(1,128)}) custom-call(f32[256,1024]{1,0:T(8,128)S(1)} %get-tuple-element.12.refs_0_, f32[4,1024]{1,0:T(4,128)S(1)} %get-tuple-element.13.refs_1_, f32[1,4]{1,0:T(1,128)S(1)} %get-tuple-element.14.refs_2_, f32[1,8]{1,0:T(1,128)S(1)} %get-tuple-element.15.refs_3_), custom_call_target="tpu_custom_call" | custom-call | tf_op jit(solution)/shard_map/pallas_call | solution.py:864
